TPU v7x, 512 devices: a whole 4x8x8 slice. The times are simulated.
512 devices in a mesh: dp: 16 (over y, core), tensor: 32 (over z, x).
Axes of the slice: x: 4, y: 8, z: 8, core: 2. Of those that a mesh axis runs over, the one named last changes fastest.
Arguments:
- x_in: bfloat16 [128, 128, 8192], P('dp', None, 'tensor'), may hold values from -16 to 16
- z_in: bfloat16 [128, 128, 8192], P('dp', None, 'tensor'), may hold values from -6 to 6
- b_in: bfloat16 [128, 128, 1024], P('dp'), may hold values from -1.5 to 1.5
- c_in: bfloat16 [128, 128, 1024], P('dp'), may hold values from -1.5 to 1.5
- dt_raw: float32 [128, 128, 128], P('dp', 'tensor'), may hold values from -4.2 to 5
- a_log: float32 [128], P('tensor'), may hold values from -3.52 to -0.91
- d_skip: float32 [128], P('tensor'), may hold values from 0.1 to 1.9
- norm_gain: float32 [8192], P('tensor'), may hold values from 0.1 to 1.9
- states: bfloat16 [128, 128, 64, 256], P('dp', 'tensor'), may hold values from -2 to 2
- dest: int32 [128], replicated, may hold values from 0 to 15, as said below
- accepted: int32 [128], replicated, may hold values from 1 to 128, as said below
Outputs:
- mixed: bfloat16 [128, 128, 8192], P('dp', None, 'tensor')
- new_states: bfloat16 [128, 128, 64, 256], P('dp', 'tensor')
Inputs may be any that keep to these rules, and one draw needn't show every extreme that they name: `dest`: every group is the destination of exactly 8 tiles. One group sends at most 1 tile to one other group, and exactly 1 to some group. The offsets (destination minus source, modulo the number of groups) that a group uses form the same set for every group; where 8 allows, that set holds half the number of groups, then 1, then minus 1. `accepted`: tile 0 and some others accept all 128 rows.
All inputs are finite; a program needn't handle non-finite values.
Results may differ from a plain program's by a relative error of at most 0.011.
Values may be sent and summed in bfloat16 or wider, within the bound.
No kernel may reach another device: no remote copies, remote signals or barrier semaphores. Data moves between devices by JAX's collectives and lax.ppermute only.
A program may use at most 64 MiB of HBM per device.

v0:
```python
import functools

import jax
import jax.numpy as jnp
from jax import lax
from jax.experimental import pallas as pl
from jax.experimental.pallas import tpu as pltpu
from jax.sharding import PartitionSpec as P

GROUPS = 4
PLACES = 16
TILES = 8
HEADS_DEV = 4
HEAD_DIM = 64
STATE = 256
ROWS = 128
WIDTH = HEADS_DEV * HEAD_DIM
TAIL = 16
MESSAGE = WIDTH + TAIL
NORM_WIDTH = 2048.0
FIXED = ((8, 0), (1, 0), (1, 1))
PAIRS = (2, 3, 4, 5, 6, 7)
MIB = 1024 * 1024
F32 = jnp.float32
BF16 = jnp.bfloat16
HBM = pl.BlockSpec(memory_space=pltpu.HBM)
VMEM = pl.BlockSpec(memory_space=pltpu.VMEM)
NN = (((1,), (0,)), ((), ()))
NT = (((1,), (1,)), ((), ()))
TN = (((0,), (0,)), ((), ()))
TABLES = [pltpu.SMEM((PLACES,), jnp.int32)] * 3
TILE_NUMBERS = pltpu.SMEM((PLACES * TILES,), jnp.int32)
HEAD_NUMBERS = pltpu.SMEM((HEADS_DEV,), F32)


def params(mib):
    return pltpu.CompilerParams(vmem_limit_bytes=mib * MIB)


def lane_ids(shape):
    return lax.broadcasted_iota(jnp.int32, shape, len(shape) - 1)


def route(dest_ref, used, sender, rank):
    me = lax.axis_index("dp")
    for o in range(PLACES):
        used[o] = 0
        sender[o] = 0
    for t in range(TILES):
        used[dest_ref[t]] = 1
        sender[lax.rem(dest_ref[me * TILES + t] - me + PLACES, PLACES)] = t
    count = 0
    for g in range(PLACES):
        o = lax.rem(me - g + PLACES, PLACES)
        rank[o] = count
        count = count + used[o]


def side_offsets(k, turn):
    if isinstance(k, int) and k == 8:
        return 8, 8
    mine = jnp.where(lax.rem(lax.axis_index("dp"), 2) == turn, k, PLACES - k)
    return mine, jnp.where(lax.rem(k, 2) == 0, mine, PLACES - mine)


def doubles(used):
    found = [jnp.int32(0), jnp.int32(0)]
    count = jnp.int32(0)
    for k in PAIRS:
        both = used[k] * used[PLACES - k]
        for n in range(2):
            found[n] = jnp.where((both == 1) & (count == n), k, found[n])
        count = count + both
    return found


def against(o):
    return lax.rem(PLACES - o, PLACES)


def step_rows(dt_ref, a_ref, rows_ref):
    for t in range(TILES):
        rows_ref[pl.ds(t * HEADS_DEV, HEADS_DEV), :] = dt_ref[t]
    raw = rows_ref[...]
    step = jnp.maximum(raw, 0.0) + jnp.log1p(jnp.exp(-jnp.abs(raw)))
    head = lax.rem(lax.broadcasted_iota(jnp.int32, raw.shape, 0), HEADS_DEV)
    a_log = jnp.zeros(raw.shape, F32)
    for h in range(HEADS_DEV):
        a_log = jnp.where(head == h, a_ref[h], a_log)
    total = -jnp.exp(a_log) * step
    lanes = lane_ids(total.shape)
    shift = 1
    while shift < ROWS:
        total = total + jnp.where(lanes >= shift, pltpu.roll(total, shift, 1), 0.0)
        shift *= 2
    return step, total


def spread_heads(columns, t):
    low = lane_ids((ROWS, 2 * HEAD_DIM)) < HEAD_DIM
    halves = []
    for j in range(2):
        at = t * HEADS_DEV + 2 * j
        halves.append(jnp.where(low, columns[:, at : at + 1], columns[:, at + 1 : at + 2]))
    return jnp.concatenate(halves, axis=1)


def group_part(ref):
    size = lax.axis_size("tensor") // GROUPS
    first = lax.div(lax.axis_index("tensor"), size) * STATE
    return ref.at[:, :, pl.ds(pl.multiple_of(first, STATE), STATE)]


def act(copies, sems, start):
    for needed, source, target, sem in copies:
        copy = pltpu.make_async_copy(source, target, sems.at[sem])
        step = copy.start if start else copy.wait
        if needed is None:
            step()
        else:
            pl.when(needed)(step)


def added_kernel(dest_hbm, accepted_hbm, a_hbm, x_hbm, b_hbm, dt_hbm, states_hbm, *rest):
    send, fixed, second = rest[0], rest[1:4], rest[4:8]
    dest_ref, accepted_ref, a_ref, x_ref, b_ref, dt_ref, rows_ref, states_ref = rest[8:16]
    added_ref, used, sender, rank, sems, out_sems = rest[16:]
    moves = (
        (dest_hbm, dest_ref),
        (accepted_hbm, accepted_ref),
        (a_hbm, a_ref),
        (dt_hbm, dt_ref),
        (states_hbm, states_ref),
        (x_hbm, x_ref),
        (group_part(b_hbm), b_ref),
    )
    loads = [pltpu.make_async_copy(*move, sems.at[i]) for i, move in enumerate(moves)]
    for load in loads:
        load.start()
    for load in loads[:4]:
        load.wait()
    route(dest_ref, used, sender, rank)
    me = lax.axis_index("dp")
    part = pl.ds(0, WIDTH)
    early, late = [], []
    for i, (k, turn) in enumerate(FIXED):
        o = side_offsets(k, turn)[0]
        early.append((None, states_ref.at[rank[against(o)]], fixed[i], PLACES + i))
    for n, k in enumerate(doubles(used)):
        for turn in (0, 1):
            o = side_offsets(k, turn)[0]
            prefix = states_ref.at[rank[against(o)]]
            early.append((k > 0, prefix, second[2 * n + turn], PLACES + 3 + 2 * n + turn))
    for to in range(PLACES):
        o = lax.rem(to - me + PLACES, PLACES)
        out, back = used[o] == 1, used[against(o)] == 1
        early.append((back & ~out, states_ref.at[rank[against(o)]], send.at[to, part, :], to))
        late.append((out, added_ref.at[sender[o]], send.at[to], to))
    loads[4].wait()
    act(early, out_sems, True)
    step, total = step_rows(dt_ref, a_ref, rows_ref)
    shape = total.shape
    lanes = lane_ids(shape)
    row_tile = lax.div(lax.broadcasted_iota(jnp.int32, shape, 0), HEADS_DEV)
    accepted = jnp.zeros(shape, jnp.int32)
    for t in range(TILES):
        accepted = jnp.where(row_tile == t, accepted_ref[me * TILES + t], accepted)
    final = jnp.sum(jnp.where(lanes == accepted - 1, total, 0.0), axis=1, keepdims=True)
    kept = lanes < accepted
    scale = jnp.where(kept, jnp.exp(jnp.where(kept, final - total, 0.0)), 0.0) * step
    columns = jnp.transpose(scale)
    fade = jnp.broadcast_to(jnp.exp(final), (shape[0], STATE))
    fade_high = fade.astype(BF16).astype(F32)
    fade_low = fade - fade_high
    empty = jnp.zeros((TAIL - 2 * HEADS_DEV, STATE), F32)
    for load in loads[5:]:
        load.wait()
    for t in range(TILES):
        x_kept = (x_ref[t].astype(F32) * spread_heads(columns, t)).astype(BF16)
        added = lax.dot_general(x_kept, b_ref[t], TN, preferred_element_type=F32)
        added_ref[t, part, :] = added.astype(BF16)
        at = t * HEADS_DEV
        tail = jnp.concatenate(
            [fade_high[at : at + HEADS_DEV], fade_low[at : at + HEADS_DEV], empty], axis=0
        )
        added_ref[t, pl.ds(WIDTH, TAIL), :] = tail.astype(BF16)
    act(late, out_sems, True)
    act(early, out_sems, False)
    act(late, out_sems, False)


def within_kernel(a_hbm, d_hbm, x_hbm, b_hbm, c_hbm, z_hbm, dt_hbm, *rest):
    out_ref, fade_ref, silu_ref, a_ref, d_ref, c_ref, x_ref, b_ref, z_ref, dt_ref = rest[:10]
    rows_ref, sems = rest[10:]
    moves = (
        (a_hbm, a_ref),
        (d_hbm, d_ref),
        (dt_hbm, dt_ref),
        (z_hbm, z_ref),
        (group_part(c_hbm), c_ref),
        (group_part(b_hbm), b_ref),
        (x_hbm, x_ref),
    )
    loads = [pltpu.make_async_copy(*move, sems.at[i]) for i, move in enumerate(moves)]
    for load in loads:
        load.start()
    for load in loads[:3]:
        load.wait()
    step, total = step_rows(dt_ref, a_ref, rows_ref)
    columns = jnp.transpose(total)
    fade_ref[...] = jnp.exp(columns)
    lower = lane_ids((ROWS, ROWS)) <= lax.broadcasted_iota(jnp.int32, (ROWS, ROWS), 0)
    wide = lax.div(lane_ids((ROWS, WIDTH)), HEAD_DIM)
    head = lax.div(lane_ids((1, WIDTH)), HEAD_DIM)
    skip = jnp.zeros((1, WIDTH), F32)
    for h in range(HEADS_DEV):
        skip = jnp.where(head == h, d_ref[h], skip)
    for load in loads[3:]:
        load.wait()
    for t in range(TILES):
        z = z_ref[t].astype(F32)
        silu_ref[t] = z / (1.0 + jnp.exp(-z))
        products = lax.dot_general(c_ref[t], b_ref[t], NT, preferred_element_type=F32)
        x = x_ref[t]
        weights = []
        inputs = []
        for h in range(HEADS_DEV):
            at = t * HEADS_DEV + h
            gap = columns[:, at : at + 1] - total[at : at + 1, :]
            decay = jnp.exp(jnp.where(lower, gap, -1e30))
            weights.append((products * decay * step[at : at + 1, :]).astype(BF16))
            inputs.append(jnp.where(wide == h, x, jnp.zeros_like(x)))
        within = lax.dot_general(
            jnp.concatenate(weights, axis=1),
            jnp.concatenate(inputs, axis=0),
            NN,
            preferred_element_type=F32,
        )
        out_ref[t] = within + skip * x.astype(F32)


def gate_kernel(dest_hbm, c_hbm, silu_hbm, within_hbm, fade_hbm, states_hbm, got, *rest):
    fixed, second = rest[:3], rest[3:7]
    gated_hbm, squares_ref, dest_ref, c_ref, silu_ref, within_ref, fade_ref = rest[7:14]
    held_ref, gated_ref, used, sender, rank, sems, held_sems, out_sems = rest[14:]
    moves = (
        (dest_hbm, dest_ref),
        (fade_hbm, fade_ref),
        (group_part(c_hbm), c_ref),
        (within_hbm, within_ref),
        (silu_hbm, silu_ref),
    )
    loads = [pltpu.make_async_copy(*move, sems.at[i]) for i, move in enumerate(moves)]
    for load in loads:
        load.start()
    loads[0].wait()
    route(dest_ref, used, sender, rank)
    part = pl.ds(0, WIDTH)
    me = lax.axis_index("dp")
    copies = [(used[0] == 1, states_hbm.at[rank[0]], sender[0])]
    for i, (k, turn) in enumerate(FIXED):
        copies.append((None, fixed[i], sender[against(side_offsets(k, turn)[1])]))
    for n, k in enumerate(doubles(used)):
        for turn in (0, 1):
            o = against(side_offsets(k, turn)[1])
            copies.append((k > 0, second[2 * n + turn], sender[o]))
    for origin in range(PLACES):
        o = lax.rem(me - origin + PLACES, PLACES)
        needed = (used[against(o)] == 1) & (used[o] == 0)
        copies.append((needed, got.at[origin, part, :], sender[against(o)]))
    copies = [(needed, source, held_ref.at[t], t) for needed, source, t in copies]
    act(copies, held_sems, True)
    for load in loads[1:]:
        load.wait()
    columns = fade_ref[...]
    lanes = lane_ids((ROWS, ROWS))
    squares = jnp.zeros((ROWS, ROWS), F32)
    outs = []
    for t in range(TILES):
        pltpu.make_async_copy(states_hbm.at[0], held_ref.at[t], held_sems.at[t]).wait()
        carried = lax.dot_general(c_ref[t], held_ref[t], NT, preferred_element_type=F32)
        total = within_ref[t] + spread_heads(columns, t) * carried
        gated = total.astype(BF16).astype(F32) * silu_ref[t]
        gated_ref[t] = gated
        outs.append(pltpu.make_async_copy(gated_ref.at[t], gated_hbm.at[t], out_sems.at[t]))
        outs[-1].start()
        squares = jnp.where(lanes == t, jnp.sum(gated * gated, axis=1, keepdims=True), squares)
    turned = jnp.transpose(squares)[:TILES]
    for i in range(squares_ref.shape[0]):
        squares_ref[i] = turned
    for out in outs:
        out.wait()


def norm_kernel(gated_hbm, squares_ref, gain_ref, out_hbm, gated_ref, out_ref, load_sems, sems):
    loads = []
    for t in range(TILES):
        loads.append(pltpu.make_async_copy(gated_hbm.at[t], gated_ref.at[t], load_sems.at[t]))
        loads[-1].start()
    total = jnp.sum(squares_ref[...], axis=0)
    factor = lax.rsqrt(total / NORM_WIDTH + 1e-05)
    filled = jnp.concatenate([factor, jnp.zeros((ROWS - TILES, ROWS), F32)], axis=0)
    columns = jnp.transpose(filled)
    gain = gain_ref[...]
    copies = []
    for t in range(TILES):
        loads[t].wait()
        out_ref[t] = (gated_ref[t] * columns[:, t : t + 1] * gain).astype(BF16)
        copies.append(pltpu.make_async_copy(out_ref.at[t], out_hbm.at[t], sems.at[t]))
        copies[-1].start()
    for copy in copies:
        copy.wait()


def state_kernel(dest_hbm, states_hbm, got, out_hbm, *rest):
    dest_ref, states_ref, held_ref, out_ref, used, sender, rank, sems, held_sems, out_sems = rest
    loads = [
        pltpu.make_async_copy(dest_hbm, dest_ref, sems.at[0]),
        pltpu.make_async_copy(states_hbm, states_ref, sems.at[1]),
    ]
    for load in loads:
        load.start()
    loads[0].wait()
    route(dest_ref, used, sender, rank)
    me = lax.axis_index("dp")
    copies = []
    for origin in range(PLACES):
        o = lax.rem(me - origin + PLACES, PLACES)
        copies.append((used[o] == 1, got.at[origin], held_ref.at[rank[o]], rank[o]))
    act(copies, held_sems, True)
    loads[1].wait()
    outs = []
    for t in range(TILES):
        pltpu.make_async_copy(got.at[0], held_ref.at[t], held_sems.at[t]).wait()
        tail = held_ref[t, pl.ds(WIDTH, TAIL), :].astype(F32)
        for h in range(HEADS_DEV):
            rows = pl.ds(h * HEAD_DIM, HEAD_DIM)
            fade = tail[h : h + 1] + tail[HEADS_DEV + h : HEADS_DEV + h + 1]
            out_ref[t, rows, :] = (
                fade * states_ref[t, rows, :].astype(F32) + held_ref[t, rows, :].astype(F32)
            ).astype(BF16)
        outs.append(pltpu.make_async_copy(out_ref.at[t], out_hbm.at[t], out_sems.at[t]))
        outs[-1].start()
    for out in outs:
        out.wait()


def shifted(message, k, turn):
    pairs = []
    for g in range(PLACES):
        forth = k if k == 8 or g % 2 == turn else PLACES - k
        pairs.append((g, (g + forth) % PLACES))
    return lax.ppermute(message, "dp", pairs)


def exchange_second(k, second):
    if k == 0:
        return tuple(jnp.zeros((WIDTH, STATE), BF16) for _ in (0, 1))
    return tuple(shifted(second[turn], k, turn) for turn in (0, 1))


def on_device(x_in, z_in, b_in, c_in, dt_raw, a_log, d_skip, norm_gain, states, dest, accepted):
    group_size = lax.axis_size("tensor") // GROUPS
    gain_row = norm_gain.reshape(1, WIDTH)
    state_rows = states.reshape(TILES, WIDTH, STATE)
    tile_shape = (TILES, ROWS, WIDTH)
    prefix = jax.ShapeDtypeStruct((WIDTH, STATE), BF16)
    messages = jax.ShapeDtypeStruct((PLACES, MESSAGE, STATE), BF16)
    state_scratch = pltpu.VMEM(state_rows.shape, BF16)
    message_scratch = pltpu.VMEM((TILES, MESSAGE, STATE), BF16)
    wide_scratch = pltpu.VMEM(tile_shape, F32)
    rows_scratch = pltpu.VMEM((TILES * HEADS_DEV, ROWS), F32)
    tile_scratch = pltpu.VMEM(tile_shape, BF16)
    dt_scratch = pltpu.VMEM(dt_raw.shape, F32)
    dma = pltpu.SemaphoreType.DMA

    pairs = jnp.array(PAIRS, jnp.int32)[:, None]
    hits = jnp.sum((dest[None, :TILES] == pairs) | (dest[None, :TILES] == PLACES - pairs), axis=1)
    both = hits == 2
    order = jnp.arange(len(PAIRS), dtype=jnp.int32)
    earlier = jnp.sum(both[None, :] & (order[None, :] < order[:, None]), axis=1)
    second_codes = [jnp.sum(jnp.where(both & (earlier == n), order + 1, 0)) for n in range(2)]

    sent = pl.pallas_call(
        added_kernel,
        in_specs=[HBM] * 7,
        out_specs=[HBM] * 8,
        out_shape=[messages] + [prefix] * 7,
        scratch_shapes=[
            TILE_NUMBERS,
            TILE_NUMBERS,
            HEAD_NUMBERS,
            tile_scratch,
            tile_scratch,
            dt_scratch,
            rows_scratch,
            state_scratch,
            message_scratch,
            *TABLES,
            dma((7,)),
            dma((PLACES + 7,)),
        ],
        compiler_params=params(54),
        name="added",
    )(dest, accepted, a_log, x_in, b_in, dt_raw, state_rows)
    send, sent_fixed, sent_second = sent[0], sent[1:4], sent[4:8]

    fixed = [shifted(value, k, turn) for value, (k, turn) in zip(sent_fixed, FIXED)]
    got = lax.all_to_all(send, "dp", split_axis=0, concat_axis=0, tiled=True)

    local = pl.pallas_call(
        within_kernel,
        in_specs=[HBM] * 7,
        out_specs=[VMEM] * 3,
        out_shape=[
            jax.ShapeDtypeStruct(tile_shape, F32),
            jax.ShapeDtypeStruct((ROWS, TILES * HEADS_DEV), F32),
            jax.ShapeDtypeStruct(tile_shape, F32),
        ],
        scratch_shapes=[
            HEAD_NUMBERS,
            HEAD_NUMBERS,
            tile_scratch,
            tile_scratch,
            tile_scratch,
            tile_scratch,
            dt_scratch,
            rows_scratch,
            dma((7,)),
        ],
        compiler_params=params(52),
        name="within",
    )(a_log, d_skip, x_in, b_in, c_in, z_in, dt_raw)

    local, sent_second, second_codes = lax.optimization_barrier((local, sent_second, second_codes))
    within, fade, silu = local
    branches = [functools.partial(exchange_second, k) for k in (0,) + PAIRS]
    later = lax.switch(second_codes[1], branches, sent_second[2:])
    second = lax.switch(second_codes[0], branches, sent_second[:2]) + later

    gated, squares = pl.pallas_call(
        gate_kernel,
        in_specs=[HBM] * 14,
        out_specs=[HBM, VMEM],
        out_shape=[
            jax.ShapeDtypeStruct(tile_shape, F32),
            jax.ShapeDtypeStruct((group_size, TILES, ROWS), F32),
        ],
        scratch_shapes=[
            TILE_NUMBERS,
            tile_scratch,
            wide_scratch,
            wide_scratch,
            pltpu.VMEM((ROWS, TILES * HEADS_DEV), F32),
            state_scratch,
            wide_scratch,
            *TABLES,
            dma((5,)),
            dma((TILES,)),
            dma((TILES,)),
        ],
        compiler_params=params(54),
        name="gate",
    )(dest, c_in, silu, within, fade, state_rows, got, *fixed, *second)

    members = [list(range(g * group_size, (g + 1) * group_size)) for g in range(GROUPS)]
    all_squares = lax.all_to_all(
        squares, "tensor", split_axis=0, concat_axis=0, axis_index_groups=members, tiled=True
    )

    new_states = pl.pallas_call(
        state_kernel,
        in_specs=[HBM] * 3,
        out_specs=HBM,
        out_shape=jax.ShapeDtypeStruct(state_rows.shape, BF16),
        scratch_shapes=[
            TILE_NUMBERS,
            state_scratch,
            message_scratch,
            state_scratch,
            *TABLES,
            dma((2,)),
            dma((TILES,)),
            dma((TILES,)),
        ],
        compiler_params=params(54),
        name="new_states",
    )(dest, state_rows, got)

    mixed = pl.pallas_call(
        norm_kernel,
        in_specs=[HBM, VMEM, VMEM],
        out_specs=HBM,
        out_shape=jax.ShapeDtypeStruct(tile_shape, BF16),
        scratch_shapes=[wide_scratch, tile_scratch, dma((TILES,)), dma((TILES,))],
        compiler_params=params(54),
        name="norm",
    )(gated, all_squares, gain_row)
    return (mixed, new_states.reshape(states.shape))


def solution(mesh):
    in_specs = (
        P("dp", None, "tensor"),
        P("dp", None, "tensor"),
        P("dp", None, None),
        P("dp", None, None),
        P("dp", "tensor", None),
        P("tensor"),
        P("tensor"),
        P("tensor"),
        P("dp", "tensor", None, None),
        P(),
        P(),
    )
    out_specs = (P("dp", None, "tensor"), P("dp", "tensor", None, None))
    return jax.shard_map(
        on_device, mesh=mesh, in_specs=in_specs, out_specs=out_specs, check_vma=False
    )
```

profile of v0, /device:TPU:136, one launch (start us, length us, event | category | flops | bytes accessed | tf_op | source)
XLA Modules:
  0.0 115.3 jit_solution(15790592812839858111)
XLA Ops:
  0.6 4.6 %added.1 = (bf16[16,272,256]{2,1,0:T(8,128)(2,1)}, bf16[256,256]{1,0:T(8,128)(2,1)}, bf16[256,256]{1,0:T(8,128)(2,1)}, bf16[256,256]{1,0:T(8,128)(2,1)}, bf16[25...) custom-call(s32[128]{0:T(128)} %dest_hbm.5, ...), custom_call_target="tpu_custom_call" | custom-call | tf_op jit(solution)/shard_map/added/pallas_call | solution.py:384
  5.3 0.0 copy-start.10
  5.3 0.0 copy-start.11
  5.3 0.0 copy-start
  5.3 0.0 copy-start.1
  5.4 7.7 %all-to-all-start = ((bf16[16,272,256]{2,1,0:T(8,128)(2,1)}), bf16[16,272,256]{2,1,0:T(8,128)(2,1)S(1)}, u32[]{:S(2)}, u32[]{:S(2)}) async-start(bf16[16,272,256]{2,1,0:T(8,128)(2,1)} %get-tuple-element.110), calls=%async_computation | async-start | bytes 4456448 | tf_op jit(solution)/shard_map/all_to_all | solution.py:409
  13.1 6.4 %collective-permute-start.24 = (bf16[256,256]{1,0:T(8,128)(2,1)}, bf16[256,256]{1,0:T(8,128)(2,1)S(1)}, u32[]{:S(2)}, u32[]{:S(2)}) collective-permute-start(bf16[256,256]{1,0:T(8,128)(2,1)} %get-tuple-element.111), channel_id=1, source_target_pairs={{0,256},{32,288},{64,320},{96,352},{128,384},{160,416},{192,448},{... | collective-permute-start | bytes 393224 | tf_op jit(solution)/shard_map/ppermute | solution.py:353
  19.4 1.9 %collective-permute-start.25 = (bf16[256,256]{1,0:T(8,128)(2,1)}, bf16[256,256]{1,0:T(8,128)(2,1)}, u32[]{:S(2)}, u32[]{:S(2)}) collective-permute-start(bf16[256,256]{1,0:T(8,128)(2,1)} %get-tuple-element.112), channel_id=1, source_target_pairs={{0,32},{32,0},{64,96},{96,64},{128,160},{160,128},{192,224},{224,1... | collective-permute-start | bytes 393224 | tf_op jit(solution)/shard_map/ppermute | solution.py:353
  21.4 3.5 %collective-permute-start.26 = (bf16[256,256]{1,0:T(8,128)(2,1)}, bf16[256,256]{1,0:T(8,128)(2,1)}, u32[]{:S(2)}, u32[]{:S(2)}) collective-permute-start(bf16[256,256]{1,0:T(8,128)(2,1)} %get-tuple-element.113), channel_id=1, source_target_pairs={{0,480},{32,64},{64,32},{96,128},{128,96},{160,192},{192,160},{224... | collective-permute-start | bytes 393224 | tf_op jit(solution)/shard_map/ppermute | solution.py:353
  24.9 0.2 convert_reduce_fusion.1
  25.1 0.1 convert_reduce_fusion
  25.2 3.7 %within.1 = (f32[8,128,256]{2,1,0:T(8,128)}, f32[128,32]{1,0:T(8,128)S(1)}, f32[8,128,256]{2,1,0:T(8,128)}) custom-call(f32[4]{0:T(128)S(1)} %copy-done.4, f32[4]{0:T(128)S(1)} %copy-done.5, bf16[8,128,256]{2,1,0:T(8,128)(2,1)S(1)} %copy-done, bf16[8,128,1024]{2,1,0:T(8,128)(2,1)} %b_hbm.3, bf16[8,128,1024]{2,1,0:T(8,128)(2,1)} %c_hbm.3, ...), custom_call_target="tpu_custom_call" | custom-call | tf_op jit(solution)/shard_map/within/pallas_call | solution.py:411
  28.9 0.6 copy-done.2
  29.6 0.7 fusion.2
  31.6 42.1 %conditional.2 = (bf16[256,256]{1,0:T(8,128)(2,1)}, bf16[256,256]{1,0:T(8,128)(2,1)}) conditional(s32[]{:T(128)} %clamp.6, () %tuple.66, (bf16[256,256]{1,0:T(8,128)(2,1)}, bf16[256,256]{1,0:T(8,128)(2,1)}) %tuple.67, (bf16[256,256]{1,0:T(8,128)(2,1)}, bf16[256,256]{1,0:T(8,128)(2,1)}) %tuple.67, ...), branch_computations={%region_4.5_spmd, %region_5.6_spmd, %region_6.7_spmd, %region_7.8_... | conditional | bytes 1048672 | solution.py:439
  31.6 2.5 %collective-permute-start = (bf16[256,256]{1,0:T(8,128)(2,1)}, bf16[256,256]{1,0:T(8,128)(2,1)}, u32[]{:S(2)}, u32[]{:S(2)}) collective-permute-start(bf16[256,256]{1,0:T(8,128)(2,1)} %get-tuple-element.48), channel_id=1, source_target_pairs={{0,64},{32,480},{64,128},{96,32},{128,192},{160,96},{192,256},{224... | collective-permute-start | bytes 393224 | tf_op jit(solution)/shard_map/cond/branch_1_fun/ppermute | solution.py:353
  34.1 3.4 %collective-permute-start.1 = (bf16[256,256]{1,0:T(8,128)(2,1)}, bf16[256,256]{1,0:T(8,128)(2,1)}, u32[]{:S(2)}, u32[]{:S(2)}) collective-permute-start(bf16[256,256]{1,0:T(8,128)(2,1)} %get-tuple-element.49), channel_id=1, source_target_pairs={{0,448},{32,96},{64,0},{96,160},{128,64},{160,224},{192,128},{224,... | collective-permute-start | bytes 393224 | tf_op jit(solution)/shard_map/cond/branch_1_fun/ppermute | solution.py:353
  37.5 33.4 %collective-permute-done = bf16[256,256]{1,0:T(8,128)(2,1)} collective-permute-done((bf16[256,256]{1,0:T(8,128)(2,1)}, bf16[256,256]{1,0:T(8,128)(2,1)}, u32[]{:S(2)}, u32[]{:S(2)}) %collective-permute-start) | collective-permute-done | bytes 131104 | tf_op jit(solution)/shard_map/cond/branch_1_fun/ppermute | solution.py:353
  70.8 2.8 %collective-permute-done.1 = bf16[256,256]{1,0:T(8,128)(2,1)} collective-permute-done((bf16[256,256]{1,0:T(8,128)(2,1)}, bf16[256,256]{1,0:T(8,128)(2,1)}, u32[]{:S(2)}, u32[]{:S(2)}) %collective-permute-start.1) | collective-permute-done | bytes 131104 | tf_op jit(solution)/shard_map/cond/branch_1_fun/ppermute | solution.py:353
  73.7 18.2 %conditional.3 = (bf16[256,256]{1,0:T(8,128)(2,1)}, bf16[256,256]{1,0:T(8,128)(2,1)}) conditional(s32[]{:T(128)} %clamp.7, () %tuple.68, (bf16[256,256]{1,0:T(8,128)(2,1)}, bf16[256,256]{1,0:T(8,128)(2,1)}) %tuple.69, (bf16[256,256]{1,0:T(8,128)(2,1)}, bf16[256,256]{1,0:T(8,128)(2,1)}) %tuple.69, ...), branch_computations={%region_11.12_spmd, %region_12.13_spmd, %region_13.14_spmd, %regio... | conditional | bytes 1048672 | solution.py:438
  73.7 5.3 %collective-permute-start.20 = (bf16[256,256]{1,0:T(8,128)(2,1)}, bf16[256,256]{1,0:T(8,128)(2,1)}, u32[]{:S(2)}, u32[]{:S(2)}) collective-permute-start(bf16[256,256]{1,0:T(8,128)(2,1)} %get-tuple-element.68), channel_id=1, source_target_pairs={{0,192},{32,352},{64,256},{96,416},{128,320},{160,480},{192,384},{... | collective-permute-start | bytes 393224 | tf_op jit(solution)/shard_map/cond/branch_5_fun/ppermute | solution.py:353
  78.9 3.6 %collective-permute-start.21 = (bf16[256,256]{1,0:T(8,128)(2,1)}, bf16[256,256]{1,0:T(8,128)(2,1)}, u32[]{:S(2)}, u32[]{:S(2)}) collective-permute-start(bf16[256,256]{1,0:T(8,128)(2,1)} %get-tuple-element.69), channel_id=1, source_target_pairs={{0,320},{32,224},{64,384},{96,288},{128,448},{160,352},{192,0},{22... | collective-permute-start | bytes 393224 | tf_op jit(solution)/shard_map/cond/branch_5_fun/ppermute | solution.py:353
  82.5 5.2 %collective-permute-done.20 = bf16[256,256]{1,0:T(8,128)(2,1)} collective-permute-done((bf16[256,256]{1,0:T(8,128)(2,1)}, bf16[256,256]{1,0:T(8,128)(2,1)}, u32[]{:S(2)}, u32[]{:S(2)}) %collective-permute-start.20) | collective-permute-done | bytes 131104 | tf_op jit(solution)/shard_map/cond/branch_5_fun/ppermute | solution.py:353
  87.7 4.2 %collective-permute-done.21 = bf16[256,256]{1,0:T(8,128)(2,1)} collective-permute-done((bf16[256,256]{1,0:T(8,128)(2,1)}, bf16[256,256]{1,0:T(8,128)(2,1)}, u32[]{:S(2)}, u32[]{:S(2)}) %collective-permute-start.21) | collective-permute-done | bytes 131104 | tf_op jit(solution)/shard_map/cond/branch_5_fun/ppermute | solution.py:353
  91.9 0.6 copy-done.7
  92.5 0.8 copy-done.6
  93.3 5.9 %gate.1 = (f32[8,128,256]{2,1,0:T(8,128)}, f32[8,8,128]{2,1,0:T(8,128)}) custom-call(s32[128]{0:T(128)} %dest_hbm.5, bf16[8,128,1024]{2,1,0:T(8,128)(2,1)} %c_hbm.3, f32[8,128,256]{2,1,0:T(8,128)} %get-tuple-element.107.silu_hbm, f32[8,128,256]{2,1,0:T(8,128)} %get-tuple-element.108.within_hbm, f32[128,32]{1,0:T(8,128)} %copy-done.2, ...), custom_call_target="tpu_custom_call" | custom-call | tf_op jit(solution)/shard_map/gate/pallas_call | solution.py:441
  99.2 6.1 %all-to-all-start.1 = ((f32[8,8,128]{2,1,0:T(8,128)}), f32[8,8,128]{2,1,0:T(8,128)S(1)}, u32[]{:S(2)}, u32[]{:S(2)}) async-start(f32[8,8,128]{2,1,0:T(8,128)} %get-tuple-element.125), calls=%async_computation.1 | async-start | bytes 65536 | tf_op jit(solution)/shard_map/all_to_all | solution.py:467
  105.3 2.9 %new_states.1 = bf16[8,256,256]{2,1,0:T(8,128)(2,1)} custom-call(s32[128]{0:T(128)} %dest_hbm.5, bf16[8,256,256]{2,1,0:T(8,128)(2,1)} %bitcast.6, bf16[16,272,256]{2,1,0:T(8,128)(2,1)} %copy-done.6), custom_call_target="tpu_custom_call" | custom-call | tf_op jit(solution)/shard_map/new_states/pallas_call | solution.py:471
  108.2 3.3 %all-to-all-done.1.squares_ref = f32[8,8,128]{2,1,0:T(8,128)S(1)} async-done(((f32[8,8,128]{2,1,0:T(8,128)}), f32[8,8,128]{2,1,0:T(8,128)S(1)}, u32[]{:S(2)}, u32[]{:S(2)}) %all-to-all-start.1) | async-done | bytes 32800 | tf_op jit(solution)/shard_map/all_to_all | solution.py:467
  111.6 0.6 copy-done.8
  112.2 3.1 %norm.1 = bf16[8,128,256]{2,1,0:T(8,128)(2,1)} custom-call(f32[8,128,256]{2,1,0:T(8,128)} %get-tuple-element.124.gated_hbm, f32[8,8,128]{2,1,0:T(8,128)} %copy-done.8, f32[1,256]{1,0:T(1,128)} %bitcast.9), custom_call_target="tpu_custom_call" | custom-call | tf_op jit(solution)/shard_map/norm/pallas_call | solution.py:490
  (21 shorter events, 0.1 us)
Async XLA Ops:
  5.3 19.6 %copy-start.9 = (s32[128]{0:T(128)S(1)}, s32[128]{0:T(128)}, u32[]{:S(2)}) copy-start(s32[128]{0:T(128)} %dest_hbm.5) | copy-start | bytes 1540
  5.3 19.6 %copy-start.10 = (s32[6]{0:T(128)S(1)}, s32[6]{0:T(128)}, u32[]{:S(2)}) copy-start(s32[6]{0:T(128)} %constant.27) | copy-start | bytes 76
  5.3 19.6 %copy-start.11 = (s32[6]{0:T(128)S(1)}, s32[6]{0:T(128)}, u32[]{:S(2)}) copy-start(s32[6]{0:T(128)} %constant.6.clone) | copy-start | bytes 76
  5.3 19.9 %copy-start = (bf16[8,128,256]{2,1,0:T(8,128)(2,1)S(1)}, bf16[8,128,256]{2,1,0:T(8,128)(2,1)}, u32[]{:S(2)}) copy-start(bf16[8,128,256]{2,1,0:T(8,128)(2,1)} %x_hbm.3) | copy-start | bytes 1572868
  5.3 19.9 %copy-start.1 = (bf16[8,128,256]{2,1,0:T(8,128)(2,1)S(1)}, bf16[8,128,256]{2,1,0:T(8,128)(2,1)}, u32[]{:S(2)}) copy-start(bf16[8,128,256]{2,1,0:T(8,128)(2,1)} %z_hbm.1) | copy-start | bytes 1572868
  5.3 19.9 %copy-start.3 = (f32[8,4,128]{2,1,0:T(4,128)S(1)}, f32[8,4,128]{2,1,0:T(4,128)}, u32[]{:S(2)}) copy-start(f32[8,4,128]{2,1,0:T(4,128)} %dt_hbm.3) | copy-start | bytes 49156
  5.4 19.9 %copy-start.4 = (f32[4]{0:T(128)S(1)}, f32[4]{0:T(128)}, u32[]{:S(2)}) copy-start(f32[4]{0:T(128)} %a_hbm.3) | copy-start | bytes 52
  5.4 19.9 %copy-start.5 = (f32[4]{0:T(128)S(1)}, f32[4]{0:T(128)}, u32[]{:S(2)}) copy-start(f32[4]{0:T(128)} %d_hbm.1) | copy-start | bytes 52
  5.4 86.5 %all-to-all-start = ((bf16[16,272,256]{2,1,0:T(8,128)(2,1)}), bf16[16,272,256]{2,1,0:T(8,128)(2,1)S(1)}, u32[]{:S(2)}, u32[]{:S(2)}) async-start(bf16[16,272,256]{2,1,0:T(8,128)(2,1)} %get-tuple-element.110), calls=%async_computation | async-start | bytes 4456448 | tf_op jit(solution)/shard_map/all_to_all | solution.py:409
  13.1 78.8 %collective-permute-start.24 = (bf16[256,256]{1,0:T(8,128)(2,1)}, bf16[256,256]{1,0:T(8,128)(2,1)S(1)}, u32[]{:S(2)}, u32[]{:S(2)}) collective-permute-start(bf16[256,256]{1,0:T(8,128)(2,1)} %get-tuple-element.111), channel_id=1, source_target_pairs={{0,256},{32,288},{64,320},{96,352},{128,384},{160,416},{192,448},{... | collective-permute-start | bytes 393224 | tf_op jit(solution)/shard_map/ppermute | solution.py:353
  19.4 72.4 %collective-permute-start.25 = (bf16[256,256]{1,0:T(8,128)(2,1)}, bf16[256,256]{1,0:T(8,128)(2,1)}, u32[]{:S(2)}, u32[]{:S(2)}) collective-permute-start(bf16[256,256]{1,0:T(8,128)(2,1)} %get-tuple-element.112), channel_id=1, source_target_pairs={{0,32},{32,0},{64,96},{96,64},{128,160},{160,128},{192,224},{224,1... | collective-permute-start | bytes 393224 | tf_op jit(solution)/shard_map/ppermute | solution.py:353
  21.4 70.5 %collective-permute-start.26 = (bf16[256,256]{1,0:T(8,128)(2,1)}, bf16[256,256]{1,0:T(8,128)(2,1)}, u32[]{:S(2)}, u32[]{:S(2)}) collective-permute-start(bf16[256,256]{1,0:T(8,128)(2,1)} %get-tuple-element.113), channel_id=1, source_target_pairs={{0,480},{32,64},{64,32},{96,128},{128,96},{160,192},{192,160},{224... | collective-permute-start | bytes 393224 | tf_op jit(solution)/shard_map/ppermute | solution.py:353
  28.9 0.6 copy-start.2
  31.6 39.2 %collective-permute-start = (bf16[256,256]{1,0:T(8,128)(2,1)}, bf16[256,256]{1,0:T(8,128)(2,1)}, u32[]{:S(2)}, u32[]{:S(2)}) collective-permute-start(bf16[256,256]{1,0:T(8,128)(2,1)} %get-tuple-element.48), channel_id=1, source_target_pairs={{0,64},{32,480},{64,128},{96,32},{128,192},{160,96},{192,256},{224... | collective-permute-start | bytes 393224 | tf_op jit(solution)/shard_map/cond/branch_1_fun/ppermute | solution.py:353
  34.1 39.6 %collective-permute-start.1 = (bf16[256,256]{1,0:T(8,128)(2,1)}, bf16[256,256]{1,0:T(8,128)(2,1)}, u32[]{:S(2)}, u32[]{:S(2)}) collective-permute-start(bf16[256,256]{1,0:T(8,128)(2,1)} %get-tuple-element.49), channel_id=1, source_target_pairs={{0,448},{32,96},{64,0},{96,160},{128,64},{160,224},{192,128},{224,... | collective-permute-start | bytes 393224 | tf_op jit(solution)/shard_map/cond/branch_1_fun/ppermute | solution.py:353
  73.7 14.0 %collective-permute-start.20 = (bf16[256,256]{1,0:T(8,128)(2,1)}, bf16[256,256]{1,0:T(8,128)(2,1)}, u32[]{:S(2)}, u32[]{:S(2)}) collective-permute-start(bf16[256,256]{1,0:T(8,128)(2,1)} %get-tuple-element.68), channel_id=1, source_target_pairs={{0,192},{32,352},{64,256},{96,416},{128,320},{160,480},{192,384},{... | collective-permute-start | bytes 393224 | tf_op jit(solution)/shard_map/cond/branch_5_fun/ppermute | solution.py:353
  78.9 12.9 %collective-permute-start.21 = (bf16[256,256]{1,0:T(8,128)(2,1)}, bf16[256,256]{1,0:T(8,128)(2,1)}, u32[]{:S(2)}, u32[]{:S(2)}) collective-permute-start(bf16[256,256]{1,0:T(8,128)(2,1)} %get-tuple-element.69), channel_id=1, source_target_pairs={{0,320},{32,224},{64,384},{96,288},{128,448},{160,352},{192,0},{22... | collective-permute-start | bytes 393224 | tf_op jit(solution)/shard_map/cond/branch_5_fun/ppermute | solution.py:353
  91.9 0.7 copy-start.7
  91.9 1.4 %copy-start.6 = (bf16[16,272,256]{2,1,0:T(8,128)(2,1)}, bf16[16,272,256]{2,1,0:T(8,128)(2,1)S(1)}, u32[]{:S(2)}) copy-start(bf16[16,272,256]{2,1,0:T(8,128)(2,1)S(1)} %all-to-all-done.got) | copy-start | bytes 6684676
  99.2 12.4 %all-to-all-start.1 = ((f32[8,8,128]{2,1,0:T(8,128)}), f32[8,8,128]{2,1,0:T(8,128)S(1)}, u32[]{:S(2)}, u32[]{:S(2)}) async-start(f32[8,8,128]{2,1,0:T(8,128)} %get-tuple-element.125), calls=%async_computation.1 | async-start | bytes 65536 | tf_op jit(solution)/shard_map/all_to_all | solution.py:467
  111.6 0.6 copy-start.8
where the time goes:
time: 116 us; the launch traced here: 115 us
  waiting for transfers between devices  48.9 us (42%)
  starting transfers between devices  40.3 us (35%)
  Pallas kernels  20.3 us (18%)
  local copies, waits for them, and re-layouts  2.65 us (2%)
  between operations  2.16 us (2%)
    ppermute x7, waiting for transfers between devices, shifted(): return lax.ppermute(message, 'dp', pairs)  45.6 us
    ppermute x7, starting transfers between devices, shifted(): return lax.ppermute(message, 'dp', pairs)  26.5 us
    all_to_all x1, starting transfers between devices, on_device(): got = lax.all_to_all(send, 'dp', split_axis=0, concat_axis=0, tiled=True)  7.69 us
    all_to_all x1, starting transfers between devices, on_device(): lax.all_to_all(squares, 'tensor', split_axis=0, concat_axis=0, axis_index...  6.12 us
    pallas_call x1, Pallas kernels, on_device(): pl.pallas_call(gate_kernel, in_specs=[HBM] * 14, out_specs=[HBM, VMEM], o...  5.88 us
    pallas_call x1, Pallas kernels, on_device(): pl.pallas_call(added_kernel, in_specs=[HBM] * 7, out_specs=[HBM] * 8, out...  4.64 us
    pallas_call x1, Pallas kernels, on_device(): pl.pallas_call(within_kernel, in_specs=[HBM] * 7, out_specs=[VMEM] * 3, o...  3.68 us
    all_to_all x1, waiting for transfers between devices, on_device(): lax.all_to_all(squares, 'tensor', split_axis=0, concat_axis=0, axis_index...  3.34 us
  transfers between devices with their start and end apart: 9, of which 5 were waited for; matrix products, arithmetic and copies ran while one was open for 1% of the time, Pallas kernels for 6%

commit v1 on v0

--- a/solution.py
+++ b/solution.py
@@ -20,9 +20,10 @@
 NORM_WIDTH = 2048.0
 FIXED = ((8, 0), (1, 0), (1, 1))
 PAIRS = (2, 3, 4, 5, 6, 7)
-MIB = 1024 * 1024
+VMEM_BYTES = 63471616
 F32 = jnp.float32
 BF16 = jnp.bfloat16
+ANY = pl.BlockSpec(memory_space=pl.ANY)
 HBM = pl.BlockSpec(memory_space=pltpu.HBM)
 VMEM = pl.BlockSpec(memory_space=pltpu.VMEM)
 NN = (((1,), (0,)), ((), ()))
@@ -33,8 +34,8 @@
 HEAD_NUMBERS = pltpu.SMEM((HEADS_DEV,), F32)
 
 
-def params(mib):
-    return pltpu.CompilerParams(vmem_limit_bytes=mib * MIB)
+def params(room=0):
+    return pltpu.CompilerParams(vmem_limit_bytes=VMEM_BYTES - room)
 
 
 def lane_ids(shape):
@@ -142,22 +143,11 @@
     route(dest_ref, used, sender, rank)
     me = lax.axis_index("dp")
     part = pl.ds(0, WIDTH)
-    early, late = [], []
-    for i, (k, turn) in enumerate(FIXED):
-        o = side_offsets(k, turn)[0]
-        early.append((None, states_ref.at[rank[against(o)]], fixed[i], PLACES + i))
-    for n, k in enumerate(doubles(used)):
-        for turn in (0, 1):
-            o = side_offsets(k, turn)[0]
-            prefix = states_ref.at[rank[against(o)]]
-            early.append((k > 0, prefix, second[2 * n + turn], PLACES + 3 + 2 * n + turn))
+    early = []
     for to in range(PLACES):
         o = lax.rem(to - me + PLACES, PLACES)
-        out, back = used[o] == 1, used[against(o)] == 1
-        early.append((back & ~out, states_ref.at[rank[against(o)]], send.at[to, part, :], to))
-        late.append((out, added_ref.at[sender[o]], send.at[to], to))
-    loads[4].wait()
-    act(early, out_sems, True)
+        needed = (used[against(o)] == 1) & (o != 0)
+        early.append((needed, states_ref.at[rank[against(o)]], send.at[to, part, :], to))
     step, total = step_rows(dt_ref, a_ref, rows_ref)
     shape = total.shape
     lanes = lane_ids(shape)
@@ -173,8 +163,11 @@
     fade_high = fade.astype(BF16).astype(F32)
     fade_low = fade - fade_high
     empty = jnp.zeros((TAIL - 2 * HEADS_DEV, STATE), F32)
+    loads[4].wait()
+    act(early, out_sems, True)
     for load in loads[5:]:
         load.wait()
+    late = []
     for t in range(TILES):
         x_kept = (x_ref[t].astype(F32) * spread_heads(columns, t)).astype(BF16)
         added = lax.dot_general(x_kept, b_ref[t], TN, preferred_element_type=F32)
@@ -184,7 +177,21 @@
             [fade_high[at : at + HEADS_DEV], fade_low[at : at + HEADS_DEV], empty], axis=0
         )
         added_ref[t, pl.ds(WIDTH, TAIL), :] = tail.astype(BF16)
-    act(late, out_sems, True)
+        to = dest_ref[me * TILES + t]
+        o = lax.rem(to - me + PLACES, PLACES)
+        late.append(((used[against(o)] == 0) | (o == 0), added_ref.at[t], send.at[to], to))
+        act(late[-1:], out_sems, True)
+    seconds = []
+    for i, (k, turn) in enumerate(FIXED):
+        o = side_offsets(k, turn)[0]
+        seconds.append((None, added_ref.at[sender[o]], fixed[i], PLACES + i))
+    for n, k in enumerate(doubles(used)):
+        for turn in (0, 1):
+            o = side_offsets(k, turn)[0]
+            i = 2 * n + turn
+            seconds.append((k > 0, added_ref.at[sender[o]], second[i], PLACES + 3 + i))
+    act(seconds, out_sems, True)
+    late += seconds
     act(early, out_sems, False)
     act(late, out_sems, False)
 
@@ -240,9 +247,9 @@
 
 
 def gate_kernel(dest_hbm, c_hbm, silu_hbm, within_hbm, fade_hbm, states_hbm, got, *rest):
-    fixed, second = rest[:3], rest[3:7]
-    gated_hbm, squares_ref, dest_ref, c_ref, silu_ref, within_ref, fade_ref = rest[7:14]
-    held_ref, gated_ref, used, sender, rank, sems, held_sems, out_sems = rest[14:]
+    gated_hbm, squares_hbm = rest[:2]
+    dest_ref, c_ref, silu_ref, within_ref, fade_ref, held_ref, gated_ref = rest[2:9]
+    squares_ref, used, sender, rank, sems, held_sems, out_sems = rest[9:]
     moves = (
         (dest_hbm, dest_ref),
         (fade_hbm, fade_ref),
@@ -258,61 +265,69 @@
     part = pl.ds(0, WIDTH)
     me = lax.axis_index("dp")
     copies = [(used[0] == 1, states_hbm.at[rank[0]], sender[0])]
-    for i, (k, turn) in enumerate(FIXED):
-        copies.append((None, fixed[i], sender[against(side_offsets(k, turn)[1])]))
-    for n, k in enumerate(doubles(used)):
-        for turn in (0, 1):
-            o = against(side_offsets(k, turn)[1])
-            copies.append((k > 0, second[2 * n + turn], sender[o]))
     for origin in range(PLACES):
         o = lax.rem(me - origin + PLACES, PLACES)
-        needed = (used[against(o)] == 1) & (used[o] == 0)
+        needed = (used[against(o)] == 1) & (o != 0)
         copies.append((needed, got.at[origin, part, :], sender[against(o)]))
     copies = [(needed, source, held_ref.at[t], t) for needed, source, t in copies]
     act(copies, held_sems, True)
     for load in loads[1:]:
         load.wait()
+    for t in range(TILES):
+        pltpu.make_async_copy(states_hbm.at[0], held_ref.at[t], held_sems.at[t]).wait()
     columns = fade_ref[...]
     lanes = lane_ids((ROWS, ROWS))
     squares = jnp.zeros((ROWS, ROWS), F32)
-    outs = []
-    for t in range(TILES):
-        pltpu.make_async_copy(states_hbm.at[0], held_ref.at[t], held_sems.at[t]).wait()
+    for t in range(TILES):
         carried = lax.dot_general(c_ref[t], held_ref[t], NT, preferred_element_type=F32)
         total = within_ref[t] + spread_heads(columns, t) * carried
         gated = total.astype(BF16).astype(F32) * silu_ref[t]
         gated_ref[t] = gated
-        outs.append(pltpu.make_async_copy(gated_ref.at[t], gated_hbm.at[t], out_sems.at[t]))
-        outs[-1].start()
         squares = jnp.where(lanes == t, jnp.sum(gated * gated, axis=1, keepdims=True), squares)
     turned = jnp.transpose(squares)[:TILES]
     for i in range(squares_ref.shape[0]):
         squares_ref[i] = turned
+    outs = [
+        pltpu.make_async_copy(squares_ref, squares_hbm, out_sems.at[0]),
+        pltpu.make_async_copy(gated_ref, gated_hbm, out_sems.at[1]),
+    ]
+    for out in outs:
+        out.start()
     for out in outs:
         out.wait()
 
 
-def norm_kernel(gated_hbm, squares_ref, gain_ref, out_hbm, gated_ref, out_ref, load_sems, sems):
-    loads = []
-    for t in range(TILES):
-        loads.append(pltpu.make_async_copy(gated_hbm.at[t], gated_ref.at[t], load_sems.at[t]))
-        loads[-1].start()
+def norm_kernel(gated_hbm, squares_hbm, gain_hbm, out_hbm, *rest):
+    gated_ref, squares_ref, gain_ref, out_ref, load_sems, sems = rest
+    half = TILES // 2
+    moves = [(squares_hbm, squares_ref), (gain_hbm, gain_ref)]
+    for j in range(2):
+        part = pl.ds(j * half, half)
+        moves.append((gated_hbm.at[part], gated_ref.at[part]))
+    loads = [pltpu.make_async_copy(*move, load_sems.at[i]) for i, move in enumerate(moves)]
+    for load in loads:
+        load.start()
+    for load in loads[:2]:
+        load.wait()
     total = jnp.sum(squares_ref[...], axis=0)
     factor = lax.rsqrt(total / NORM_WIDTH + 1e-05)
     filled = jnp.concatenate([factor, jnp.zeros((ROWS - TILES, ROWS), F32)], axis=0)
     columns = jnp.transpose(filled)
     gain = gain_ref[...]
     copies = []
-    for t in range(TILES):
-        loads[t].wait()
-        out_ref[t] = (gated_ref[t] * columns[:, t : t + 1] * gain).astype(BF16)
-        copies.append(pltpu.make_async_copy(out_ref.at[t], out_hbm.at[t], sems.at[t]))
+    for j in range(2):
+        loads[2 + j].wait()
+        for t in range(j * half, (j + 1) * half):
+            out_ref[t] = (gated_ref[t] * columns[:, t : t + 1] * gain).astype(BF16)
+        part = pl.ds(j * half, half)
+        copies.append(pltpu.make_async_copy(out_ref.at[part], out_hbm.at[part], sems.at[j]))
         copies[-1].start()
     for copy in copies:
         copy.wait()
 
 
-def state_kernel(dest_hbm, states_hbm, got, out_hbm, *rest):
+def state_kernel(dest_hbm, states_hbm, got, *rest):
+    fixed, second, out_hbm, rest = rest[:3], rest[3:7], rest[7], rest[8:]
     dest_ref, states_ref, held_ref, out_ref, used, sender, rank, sems, held_sems, out_sems = rest
     loads = [
         pltpu.make_async_copy(dest_hbm, dest_ref, sems.at[0]),
@@ -324,9 +339,17 @@
     route(dest_ref, used, sender, rank)
     me = lax.axis_index("dp")
     copies = []
+    for i, (k, turn) in enumerate(FIXED):
+        slot = rank[side_offsets(k, turn)[1]]
+        copies.append((None, fixed[i], held_ref.at[slot], slot))
+    for n, k in enumerate(doubles(used)):
+        for turn in (0, 1):
+            slot = rank[side_offsets(k, turn)[1]]
+            copies.append((k > 0, second[2 * n + turn], held_ref.at[slot], slot))
     for origin in range(PLACES):
         o = lax.rem(me - origin + PLACES, PLACES)
-        copies.append((used[o] == 1, got.at[origin], held_ref.at[rank[o]], rank[o]))
+        needed = (used[o] == 1) & ((used[against(o)] == 0) | (o == 0))
+        copies.append((needed, got.at[origin], held_ref.at[rank[o]], rank[o]))
     act(copies, held_sems, True)
     loads[1].wait()
     outs = []
@@ -355,7 +378,7 @@
 
 def exchange_second(k, second):
     if k == 0:
-        return tuple(jnp.zeros((WIDTH, STATE), BF16) for _ in (0, 1))
+        return tuple(jnp.zeros((MESSAGE, STATE), BF16) for _ in (0, 1))
     return tuple(shifted(second[turn], k, turn) for turn in (0, 1))
 
 
@@ -364,7 +387,7 @@
     gain_row = norm_gain.reshape(1, WIDTH)
     state_rows = states.reshape(TILES, WIDTH, STATE)
     tile_shape = (TILES, ROWS, WIDTH)
-    prefix = jax.ShapeDtypeStruct((WIDTH, STATE), BF16)
+    message = jax.ShapeDtypeStruct((MESSAGE, STATE), BF16)
     messages = jax.ShapeDtypeStruct((PLACES, MESSAGE, STATE), BF16)
     state_scratch = pltpu.VMEM(state_rows.shape, BF16)
     message_scratch = pltpu.VMEM((TILES, MESSAGE, STATE), BF16)
@@ -385,7 +408,7 @@
         added_kernel,
         in_specs=[HBM] * 7,
         out_specs=[HBM] * 8,
-        out_shape=[messages] + [prefix] * 7,
+        out_shape=[messages] + [message] * 7,
         scratch_shapes=[
             TILE_NUMBERS,
             TILE_NUMBERS,
@@ -400,7 +423,7 @@
             dma((7,)),
             dma((PLACES + 7,)),
         ],
-        compiler_params=params(54),
+        compiler_params=params(),
         name="added",
     )(dest, accepted, a_log, x_in, b_in, dt_raw, state_rows)
     send, sent_fixed, sent_second = sent[0], sent[1:4], sent[4:8]
@@ -428,7 +451,7 @@
             rows_scratch,
             dma((7,)),
         ],
-        compiler_params=params(52),
+        compiler_params=params(),
         name="within",
     )(a_log, d_skip, x_in, b_in, c_in, z_in, dt_raw)
 
@@ -436,12 +459,14 @@
     within, fade, silu = local
     branches = [functools.partial(exchange_second, k) for k in (0,) + PAIRS]
     later = lax.switch(second_codes[1], branches, sent_second[2:])
+    later, sent_second = lax.optimization_barrier((later, sent_second))
     second = lax.switch(second_codes[0], branches, sent_second[:2]) + later
+    within, second = lax.optimization_barrier((within, second))
 
     gated, squares = pl.pallas_call(
         gate_kernel,
-        in_specs=[HBM] * 14,
-        out_specs=[HBM, VMEM],
+        in_specs=[HBM] * 6 + [ANY],
+        out_specs=[HBM] * 2,
         out_shape=[
             jax.ShapeDtypeStruct(tile_shape, F32),
             jax.ShapeDtypeStruct((group_size, TILES, ROWS), F32),
@@ -454,14 +479,15 @@
             pltpu.VMEM((ROWS, TILES * HEADS_DEV), F32),
             state_scratch,
             wide_scratch,
+            pltpu.VMEM((group_size, TILES, ROWS), F32),
             *TABLES,
             dma((5,)),
             dma((TILES,)),
-            dma((TILES,)),
-        ],
-        compiler_params=params(54),
+            dma((2,)),
+        ],
+        compiler_params=params(4500000),
         name="gate",
-    )(dest, c_in, silu, within, fade, state_rows, got, *fixed, *second)
+    )(dest, c_in, silu, within, fade, state_rows, got)
 
     members = [list(range(g * group_size, (g + 1) * group_size)) for g in range(GROUPS)]
     all_squares = lax.all_to_all(
@@ -470,7 +496,7 @@
 
     new_states = pl.pallas_call(
         state_kernel,
-        in_specs=[HBM] * 3,
+        in_specs=[HBM] * 2 + [ANY] * 8,
         out_specs=HBM,
         out_shape=jax.ShapeDtypeStruct(state_rows.shape, BF16),
         scratch_shapes=[
@@ -483,17 +509,24 @@
             dma((TILES,)),
             dma((TILES,)),
         ],
-        compiler_params=params(54),
+        compiler_params=params(4500000),
         name="new_states",
-    )(dest, state_rows, got)
+    )(dest, state_rows, got, *fixed, *second)
 
     mixed = pl.pallas_call(
         norm_kernel,
-        in_specs=[HBM, VMEM, VMEM],
+        in_specs=[HBM, ANY, HBM],
         out_specs=HBM,
         out_shape=jax.ShapeDtypeStruct(tile_shape, BF16),
-        scratch_shapes=[wide_scratch, tile_scratch, dma((TILES,)), dma((TILES,))],
-        compiler_params=params(54),
+        scratch_shapes=[
+            wide_scratch,
+            pltpu.VMEM((group_size, TILES, ROWS), F32),
+            pltpu.VMEM((1, WIDTH), F32),
+            tile_scratch,
+            dma((4,)),
+            dma((2,)),
+        ],
+        compiler_params=params(400000),
         name="norm",
     )(gated, all_squares, gain_row)
     return (mixed, new_states.reshape(states.shape))

time: 116 us -> 87 us (0.75)
  the two profiles are of different devices: /device:TPU:136 before, /device:TPU:32 now
where the time goes in v1:
time: 87 us; the launch traced here: 86.5 us
  waiting for transfers between devices  36.7 us (42%)
  starting transfers between devices  23 us (26%)
  Pallas kernels  17.8 us (20%)
  local copies, waits for them, and re-layouts  6.03 us (7%)
  between operations  2.01 us (2%)
  other arithmetic  0.98 us (1%)
    all_to_all x1, waiting for transfers between devices, on_device(): got = lax.all_to_all(send, 'dp', split_axis=0, concat_axis=0, tiled=True)  34.8 us
    all_to_all x1, starting transfers between devices, on_device(): got = lax.all_to_all(send, 'dp', split_axis=0, concat_axis=0, tiled=True)  9.19 us
    ppermute x3, starting transfers between devices, shifted(): return lax.ppermute(message, 'dp', pairs)  9.12 us
    pallas_call x1, Pallas kernels, on_device(): pl.pallas_call(gate_kernel, in_specs=[HBM] * 6 + [ANY], out_specs=[HBM] *...  4.72 us
    all_to_all x1, starting transfers between devices, on_device(): lax.all_to_all(squares, 'tensor', split_axis=0, concat_axis=0, axis_index...  4.66 us
    pallas_call x1, Pallas kernels, on_device(): pl.pallas_call(added_kernel, in_specs=[HBM] * 7, out_specs=[HBM] * 8, out...  3.98 us
    pallas_call x1, Pallas kernels, on_device(): pl.pallas_call(within_kernel, in_specs=[HBM] * 7, out_specs=[VMEM] * 3, o...  3.97 us
    unnamed x22, local copies, waits for them, and re-layouts  3.36 us
  transfers between devices with their start and end apart: 5, of which 2 were waited for; matrix products, arithmetic and copies ran while one was open for 4% of the time, Pallas kernels for 14%

profile of v1, /device:TPU:32, one launch (start us, length us, event | category | flops | bytes accessed | tf_op | source)
XLA Modules:
  0.0 86.5 jit_solution(7984561526667312369)
XLA Ops:
  0.6 4.0 %added.1 = (bf16[16,272,256]{2,1,0:T(8,128)(2,1)}, bf16[272,256]{1,0:T(8,128)(2,1)}, bf16[272,256]{1,0:T(8,128)(2,1)}, bf16[272,256]{1,0:T(8,128)(2,1)}, bf16[27...) custom-call(s32[128]{0:T(128)} %dest_hbm.5, ...), custom_call_target="tpu_custom_call" | custom-call | tf_op jit(solution)/shard_map/added/pallas_call | solution.py:407
  4.6 0.0 copy-start.10
  4.6 0.0 copy-start.9
  4.7 9.2 %all-to-all-start = ((bf16[16,272,256]{2,1,0:T(8,128)(2,1)}), bf16[16,272,256]{2,1,0:T(8,128)(2,1)S(1)}, u32[]{:S(2)}, u32[]{:S(2)}) async-start(bf16[16,272,256]{2,1,0:T(8,128)(2,1)} %get-tuple-element.134), calls=%async_computation | async-start | bytes 4456448 | tf_op jit(solution)/shard_map/all_to_all | solution.py:432
  13.8 2.1 %collective-permute-start.24 = (bf16[272,256]{1,0:T(8,128)(2,1)S(1)}, bf16[272,256]{1,0:T(8,128)(2,1)S(1)}, u32[]{:S(2)}, u32[]{:S(2)}) collective-permute-start(bf16[272,256]{1,0:T(8,128)(2,1)S(1)} %copy-done.10), channel_id=1, source_target_pairs={{0,256},{32,288},{64,320},{96,352},{128,384},{160,416},{192,448},{... | collective-permute-start | bytes 417800 | tf_op jit(solution)/shard_map/ppermute | solution.py:376
  15.9 1.9 %collective-permute-start.25 = (bf16[272,256]{1,0:T(8,128)(2,1)S(1)}, bf16[272,256]{1,0:T(8,128)(2,1)S(1)}, u32[]{:S(2)}, u32[]{:S(2)}) collective-permute-start(bf16[272,256]{1,0:T(8,128)(2,1)S(1)} %copy-done.9), channel_id=1, source_target_pairs={{0,32},{32,0},{64,96},{96,64},{128,160},{160,128},{192,224},{224,1... | collective-permute-start | bytes 417800 | tf_op jit(solution)/shard_map/ppermute | solution.py:376
  17.9 5.1 %collective-permute-start.26 = (bf16[272,256]{1,0:T(8,128)(2,1)S(1)}, bf16[272,256]{1,0:T(8,128)(2,1)S(1)}, u32[]{:S(2)}, u32[]{:S(2)}) collective-permute-start(bf16[272,256]{1,0:T(8,128)(2,1)S(1)} %copy-done.8), channel_id=1, source_target_pairs={{0,480},{32,64},{64,32},{96,128},{128,96},{160,192},{192,160},{224... | collective-permute-start | bytes 417800 | tf_op jit(solution)/shard_map/ppermute | solution.py:376
  23.0 0.0 copy-start.5
  23.0 0.0 copy-start.6
  23.0 0.0 copy-start.7
  23.0 4.0 %within.1 = (f32[8,128,256]{2,1,0:T(8,128)}, f32[128,32]{1,0:T(8,128)}, f32[8,128,256]{2,1,0:T(8,128)}) custom-call(f32[4]{0:T(128)} %a_hbm.3, f32[4]{0:T(128)} %d_hbm.1, bf16[8,128,256]{2,1,0:T(8,128)(2,1)} %x_hbm.3, bf16[8,128,1024]{2,1,0:T(8,128)(2,1)} %b_hbm.3, bf16[8,128,1024]{2,1,0:T(8,128)(2,1)} %c_hbm.3, bf16[8,128,256]{2,1,0:T(8,128)(2,1)} %z_hbm.1, ...), custom_call_target="tpu_custom_call" | custom-call | tf_op jit(solution)/shard_map/within/pallas_call | solution.py:434
  27.0 0.2 convert_reduce_fusion.1
  27.2 0.1 convert_reduce_fusion
  27.4 0.7 fusion.2
  29.2 1.4 %conditional.2 = (bf16[272,256]{1,0:T(8,128)(2,1)}, bf16[272,256]{1,0:T(8,128)(2,1)}) conditional(s32[]{:T(128)} %clamp.7, () %tuple.69, (bf16[272,256]{1,0:T(8,128)(2,1)S(1)}, bf16[272,256]{1,0:T(8,128)(2,1)}) %tuple.70, (bf16[272,256]{1,0:T(8,128)(2,1)S(1)}, bf16[272,256]{1,0:T(8,128)(2,1)}) %tuple.70, ...), branch_computations={%region_4.5_spmd, %region_5.6_spmd, %region_6.7_spmd, %region_7.8_... | conditional | bytes 1114208 | solution.py:461
  29.2 0.7 broadcast.20
  29.9 0.7 broadcast.20.clone
  30.6 1.3 %conditional.3 = (bf16[272,256]{1,0:T(8,128)(2,1)}, bf16[272,256]{1,0:T(8,128)(2,1)}) conditional(s32[]{:T(128)} %clamp.6, () %tuple.68, (bf16[272,256]{1,0:T(8,128)(2,1)S(1)}, bf16[272,256]{1,0:T(8,128)(2,1)S(1)}) %tuple.72, (bf16[272,256]{1,0:T(8,128)(2,1)S(1)}, bf16[272,256]{1,0:T(8,128)(2,1)S(1)}) %tuple.72, ...), branch_computations={%region_11.12_spmd, %region_12.13_spmd, %region_13.14_spmd, %regio... | conditional | bytes 1114208 | solution.py:463
  30.6 0.7 broadcast.21
  31.2 0.7 broadcast.21.clone
  31.9 34.8 %all-to-all-done.got = bf16[16,272,256]{2,1,0:T(8,128)(2,1)S(1)} async-done(((bf16[16,272,256]{2,1,0:T(8,128)(2,1)}), bf16[16,272,256]{2,1,0:T(8,128)(2,1)S(1)}, u32[]{:S(2)}, u32[]{:S(2)}) %all-to-all-start) | async-done | bytes 2228256 | tf_op jit(solution)/shard_map/all_to_all | solution.py:432
  66.8 1.4 %copy-done = bf16[16,272,256]{2,1,0:T(8,128)(2,1)} copy-done((bf16[16,272,256]{2,1,0:T(8,128)(2,1)}, bf16[16,272,256]{2,1,0:T(8,128)(2,1)S(1)}, u32[]{:S(2)}) %copy-start) | copy-done | bytes 2228248
  68.1 4.7 %gate.1 = (f32[8,128,256]{2,1,0:T(8,128)}, f32[8,8,128]{2,1,0:T(8,128)}) custom-call(s32[128]{0:T(128)} %dest_hbm.5, bf16[8,128,1024]{2,1,0:T(8,128)(2,1)} %c_hbm.3, f32[8,128,256]{2,1,0:T(8,128)} %get-tuple-element.116.silu_hbm, f32[8,128,256]{2,1,0:T(8,128)} %get-tuple-element.132.within_hbm, f32[128,32]{1,0:T(8,128)} %get-tuple-element.133.fade_hbm, ...), custom_call_target="tpu_custom_call" | custom-call | tf_op jit(solution)/shard_map/gate/pallas_call | solution.py:466
  72.9 4.7 %all-to-all-start.1 = ((f32[8,8,128]{2,1,0:T(8,128)}), f32[8,8,128]{2,1,0:T(8,128)S(1)}, u32[]{:S(2)}, u32[]{:S(2)}) async-start(f32[8,8,128]{2,1,0:T(8,128)} %get-tuple-element.136), calls=%async_computation.1 | async-start | bytes 65536 | tf_op jit(solution)/shard_map/all_to_all | solution.py:493
  77.5 0.0 copy-start.1
  77.6 0.6 copy-done.1
  78.2 0.0 copy-done.2
  78.2 0.7 copy-done.3
  78.9 3.0 %new_states.1 = bf16[8,256,256]{2,1,0:T(8,128)(2,1)} custom-call(s32[128]{0:T(128)} %dest_hbm.5, bf16[8,256,256]{2,1,0:T(8,128)(2,1)} %bitcast.6, bf16[16,272,256]{2,1,0:T(8,128)(2,1)} %copy-done, bf16[272,256]{1,0:T(8,128)(2,1)} %copy-done.1, bf16[272,256]{1,0:T(8,128)(2,1)} %copy-done.2, bf16[272,256]{1,0:T(8,128)(2,1)} %copy-done.3, ...), custom_call_target="tpu_custom_call" | custom-call | tf_op jit(solution)/shard_map/new_states/pallas_call | solution.py:497
  81.9 1.9 %all-to-all-done.1.squares_hbm = f32[8,8,128]{2,1,0:T(8,128)S(1)} async-done(((f32[8,8,128]{2,1,0:T(8,128)}), f32[8,8,128]{2,1,0:T(8,128)S(1)}, u32[]{:S(2)}, u32[]{:S(2)}) %all-to-all-start.1) | async-done | bytes 32800 | tf_op jit(solution)/shard_map/all_to_all | solution.py:493
  83.8 0.6 copy-done.4
  84.4 2.1 %norm.1 = bf16[8,128,256]{2,1,0:T(8,128)(2,1)} custom-call(f32[8,128,256]{2,1,0:T(8,128)} %get-tuple-element.135.gated_hbm, f32[8,8,128]{2,1,0:T(8,128)} %copy-done.4, f32[1,256]{1,0:T(1,128)} %bitcast.9), custom_call_target="tpu_custom_call" | custom-call | tf_op jit(solution)/shard_map/norm/pallas_call | solution.py:516
  (15 shorter events, 0.0 us)
Async XLA Ops:
  4.6 9.2 %copy-start.10 = (bf16[272,256]{1,0:T(8,128)(2,1)S(1)}, bf16[272,256]{1,0:T(8,128)(2,1)}, u32[]{:S(2)}) copy-start(bf16[272,256]{1,0:T(8,128)(2,1)} %get-tuple-element.137) | copy-start | bytes 417796
  4.6 11.3 %copy-start.9 = (bf16[272,256]{1,0:T(8,128)(2,1)S(1)}, bf16[272,256]{1,0:T(8,128)(2,1)}, u32[]{:S(2)}) copy-start(bf16[272,256]{1,0:T(8,128)(2,1)} %get-tuple-element.138) | copy-start | bytes 417796
  4.6 13.2 %copy-start.8 = (bf16[272,256]{1,0:T(8,128)(2,1)S(1)}, bf16[272,256]{1,0:T(8,128)(2,1)}, u32[]{:S(2)}) copy-start(bf16[272,256]{1,0:T(8,128)(2,1)} %get-tuple-element.139) | copy-start | bytes 417796
  4.7 62.1 %all-to-all-start = ((bf16[16,272,256]{2,1,0:T(8,128)(2,1)}), bf16[16,272,256]{2,1,0:T(8,128)(2,1)S(1)}, u32[]{:S(2)}, u32[]{:S(2)}) async-start(bf16[16,272,256]{2,1,0:T(8,128)(2,1)} %get-tuple-element.134), calls=%async_computation | async-start | bytes 4456448 | tf_op jit(solution)/shard_map/all_to_all | solution.py:432
  13.8 63.7 %collective-permute-start.24 = (bf16[272,256]{1,0:T(8,128)(2,1)S(1)}, bf16[272,256]{1,0:T(8,128)(2,1)S(1)}, u32[]{:S(2)}, u32[]{:S(2)}) collective-permute-start(bf16[272,256]{1,0:T(8,128)(2,1)S(1)} %copy-done.10), channel_id=1, source_target_pairs={{0,256},{32,288},{64,320},{96,352},{128,384},{160,416},{192,448},{... | collective-permute-start | bytes 417800 | tf_op jit(solution)/shard_map/ppermute | solution.py:376
  15.9 61.6 %collective-permute-start.25 = (bf16[272,256]{1,0:T(8,128)(2,1)S(1)}, bf16[272,256]{1,0:T(8,128)(2,1)S(1)}, u32[]{:S(2)}, u32[]{:S(2)}) collective-permute-start(bf16[272,256]{1,0:T(8,128)(2,1)S(1)} %copy-done.9), channel_id=1, source_target_pairs={{0,32},{32,0},{64,96},{96,64},{128,160},{160,128},{192,224},{224,1... | collective-permute-start | bytes 417800 | tf_op jit(solution)/shard_map/ppermute | solution.py:376
  17.9 59.7 %collective-permute-start.26 = (bf16[272,256]{1,0:T(8,128)(2,1)S(1)}, bf16[272,256]{1,0:T(8,128)(2,1)S(1)}, u32[]{:S(2)}, u32[]{:S(2)}) collective-permute-start(bf16[272,256]{1,0:T(8,128)(2,1)S(1)} %copy-done.8), channel_id=1, source_target_pairs={{0,480},{32,64},{64,32},{96,128},{128,96},{160,192},{192,160},{224... | collective-permute-start | bytes 417800 | tf_op jit(solution)/shard_map/ppermute | solution.py:376
  23.0 4.0 %copy-start.5 = (s32[128]{0:T(128)S(1)}, s32[128]{0:T(128)}, u32[]{:S(2)}) copy-start(s32[128]{0:T(128)} %dest_hbm.5) | copy-start | bytes 1540
  23.0 4.0 %copy-start.6 = (s32[6]{0:T(128)S(1)}, s32[6]{0:T(128)}, u32[]{:S(2)}) copy-start(s32[6]{0:T(128)} %constant.27) | copy-start | bytes 76
  23.0 4.0 %copy-start.7 = (s32[6]{0:T(128)S(1)}, s32[6]{0:T(128)}, u32[]{:S(2)}) copy-start(s32[6]{0:T(128)} %constant.6.clone) | copy-start | bytes 76
  66.8 1.4 %copy-start = (bf16[16,272,256]{2,1,0:T(8,128)(2,1)}, bf16[16,272,256]{2,1,0:T(8,128)(2,1)S(1)}, u32[]{:S(2)}) copy-start(bf16[16,272,256]{2,1,0:T(8,128)(2,1)S(1)} %all-to-all-done.got) | copy-start | bytes 6684676
  72.9 10.9 %all-to-all-start.1 = ((f32[8,8,128]{2,1,0:T(8,128)}), f32[8,8,128]{2,1,0:T(8,128)S(1)}, u32[]{:S(2)}, u32[]{:S(2)}) async-start(f32[8,8,128]{2,1,0:T(8,128)} %get-tuple-element.136), calls=%async_computation.1 | async-start | bytes 65536 | tf_op jit(solution)/shard_map/all_to_all | solution.py:493
  77.5 0.7 copy-start.1
  77.6 0.7 copy-start.2
  78.2 0.7 copy-start.3
  83.8 0.6 copy-start.4

commit v2 on v1

--- a/solution.py
+++ b/solution.py
@@ -123,9 +123,9 @@
 
 
 def added_kernel(dest_hbm, accepted_hbm, a_hbm, x_hbm, b_hbm, dt_hbm, states_hbm, *rest):
-    send, fixed, second = rest[0], rest[1:4], rest[4:8]
-    dest_ref, accepted_ref, a_ref, x_ref, b_ref, dt_ref, rows_ref, states_ref = rest[8:16]
-    added_ref, used, sender, rank, sems, out_sems = rest[16:]
+    send, fixed, second, codes = rest[0], rest[1:4], rest[4:8], rest[8:10]
+    dest_ref, accepted_ref, a_ref, x_ref, b_ref, dt_ref, rows_ref, states_ref = rest[10:18]
+    added_ref, used, sender, rank, sems, out_sems = rest[18:]
     moves = (
         (dest_hbm, dest_ref),
         (accepted_hbm, accepted_ref),
@@ -186,6 +186,7 @@
         o = side_offsets(k, turn)[0]
         seconds.append((None, added_ref.at[sender[o]], fixed[i], PLACES + i))
     for n, k in enumerate(doubles(used)):
+        codes[n][0] = jnp.maximum(k - 1, 0)
         for turn in (0, 1):
             o = side_offsets(k, turn)[0]
             i = 2 * n + turn
@@ -382,13 +383,11 @@
     return tuple(shifted(second[turn], k, turn) for turn in (0, 1))
 
 
-def on_device(x_in, z_in, b_in, c_in, dt_raw, a_log, d_skip, norm_gain, states, dest, accepted):
+def finish(first_pair, code, sent, arrays):
+    x_in, z_in, b_in, c_in, dt_raw, a_log, d_skip, gain_row, state_rows, dest = arrays
+    send, sent_fixed, sent_second = sent[0], sent[1:4], tuple(sent[4:8])
     group_size = lax.axis_size("tensor") // GROUPS
-    gain_row = norm_gain.reshape(1, WIDTH)
-    state_rows = states.reshape(TILES, WIDTH, STATE)
     tile_shape = (TILES, ROWS, WIDTH)
-    message = jax.ShapeDtypeStruct((MESSAGE, STATE), BF16)
-    messages = jax.ShapeDtypeStruct((PLACES, MESSAGE, STATE), BF16)
     state_scratch = pltpu.VMEM(state_rows.shape, BF16)
     message_scratch = pltpu.VMEM((TILES, MESSAGE, STATE), BF16)
     wide_scratch = pltpu.VMEM(tile_shape, F32)
@@ -396,37 +395,6 @@
     tile_scratch = pltpu.VMEM(tile_shape, BF16)
     dt_scratch = pltpu.VMEM(dt_raw.shape, F32)
     dma = pltpu.SemaphoreType.DMA
-
-    pairs = jnp.array(PAIRS, jnp.int32)[:, None]
-    hits = jnp.sum((dest[None, :TILES] == pairs) | (dest[None, :TILES] == PLACES - pairs), axis=1)
-    both = hits == 2
-    order = jnp.arange(len(PAIRS), dtype=jnp.int32)
-    earlier = jnp.sum(both[None, :] & (order[None, :] < order[:, None]), axis=1)
-    second_codes = [jnp.sum(jnp.where(both & (earlier == n), order + 1, 0)) for n in range(2)]
-
-    sent = pl.pallas_call(
-        added_kernel,
-        in_specs=[HBM] * 7,
-        out_specs=[HBM] * 8,
-        out_shape=[messages] + [message] * 7,
-        scratch_shapes=[
-            TILE_NUMBERS,
-            TILE_NUMBERS,
-            HEAD_NUMBERS,
-            tile_scratch,
-            tile_scratch,
-            dt_scratch,
-            rows_scratch,
-            state_scratch,
-            message_scratch,
-            *TABLES,
-            dma((7,)),
-            dma((PLACES + 7,)),
-        ],
-        compiler_params=params(),
-        name="added",
-    )(dest, accepted, a_log, x_in, b_in, dt_raw, state_rows)
-    send, sent_fixed, sent_second = sent[0], sent[1:4], sent[4:8]
 
     fixed = [shifted(value, k, turn) for value, (k, turn) in zip(sent_fixed, FIXED)]
     got = lax.all_to_all(send, "dp", split_axis=0, concat_axis=0, tiled=True)
@@ -455,13 +423,18 @@
         name="within",
     )(a_log, d_skip, x_in, b_in, c_in, z_in, dt_raw)
 
-    local, sent_second, second_codes = lax.optimization_barrier((local, sent_second, second_codes))
+    if first_pair:
+        second = exchange_second(first_pair, sent_second[:2])
+        rest = (0,) + tuple(k for k in PAIRS if k > first_pair)
+        branches = [functools.partial(exchange_second, k) for k in rest]
+        inner = jnp.where(code > 0, code - first_pair + 1, 0)
+        sent_second, local = lax.optimization_barrier((sent_second, local))
+        later = lax.switch(inner, branches, sent_second[2:])
+        local, later = lax.optimization_barrier((local, later))
+        second += later
+    else:
+        second = sent_second
     within, fade, silu = local
-    branches = [functools.partial(exchange_second, k) for k in (0,) + PAIRS]
-    later = lax.switch(second_codes[1], branches, sent_second[2:])
-    later, sent_second = lax.optimization_barrier((later, sent_second))
-    second = lax.switch(second_codes[0], branches, sent_second[:2]) + later
-    within, second = lax.optimization_barrier((within, second))
 
     gated, squares = pl.pallas_call(
         gate_kernel,
@@ -529,6 +502,50 @@
         compiler_params=params(400000),
         name="norm",
     )(gated, all_squares, gain_row)
+    return (mixed, new_states)
+
+
+def on_device(x_in, z_in, b_in, c_in, dt_raw, a_log, d_skip, norm_gain, states, dest, accepted):
+    gain_row = norm_gain.reshape(1, WIDTH)
+    state_rows = states.reshape(TILES, WIDTH, STATE)
+    tile_shape = (TILES, ROWS, WIDTH)
+    message = jax.ShapeDtypeStruct((MESSAGE, STATE), BF16)
+    messages = jax.ShapeDtypeStruct((PLACES, MESSAGE, STATE), BF16)
+    state_scratch = pltpu.VMEM(state_rows.shape, BF16)
+    message_scratch = pltpu.VMEM((TILES, MESSAGE, STATE), BF16)
+    rows_scratch = pltpu.VMEM((TILES * HEADS_DEV, ROWS), F32)
+    tile_scratch = pltpu.VMEM(tile_shape, BF16)
+    dt_scratch = pltpu.VMEM(dt_raw.shape, F32)
+    dma = pltpu.SemaphoreType.DMA
+
+    sent = pl.pallas_call(
+        added_kernel,
+        in_specs=[HBM] * 7,
+        out_specs=[HBM] * 8 + [pl.BlockSpec(memory_space=pltpu.SMEM)] * 2,
+        out_shape=[messages] + [message] * 7 + [jax.ShapeDtypeStruct((1,), jnp.int32)] * 2,
+        scratch_shapes=[
+            TILE_NUMBERS,
+            TILE_NUMBERS,
+            HEAD_NUMBERS,
+            tile_scratch,
+            tile_scratch,
+            dt_scratch,
+            rows_scratch,
+            state_scratch,
+            message_scratch,
+            *TABLES,
+            dma((7,)),
+            dma((PLACES + 7,)),
+        ],
+        compiler_params=params(),
+        name="added",
+    )(dest, accepted, a_log, x_in, b_in, dt_raw, state_rows)
+    *sent, first_code, second_code = sent
+    arrays = (x_in, z_in, b_in, c_in, dt_raw, a_log, d_skip, gain_row, state_rows, dest)
+    branches = [functools.partial(finish, k) for k in (0,) + PAIRS]
+    mixed, new_states = lax.switch(
+        first_code.reshape(()), branches, second_code.reshape(()), sent, arrays
+    )
     return (mixed, new_states.reshape(states.shape))
 
 

time: 87 us -> 87.7 us (level)
  waiting for transfers between devices: 36.7 us -> 43.2 us
  local copies, waits for them, and re-layouts: 6.03 us -> 0.63 us
  other arithmetic: 0.98 us -> 0 us
    all_to_all x2, waiting for transfers between devices: 36.7 us -> 43.2 us  [the longest x1 40 us: finish(): got = lax.all_to_all(send, 'dp', split_axis=0, concat_axis=0, tiled=True)]
    unnamed x22 -> x14, local copies, waits for them, and re-layouts: 3.36 us -> 0.03 us
    another operation x4 -> x0, local copies, waits for them, and re-layouts: 2.66 us -> none
    reduce_sum x3 -> x0, other arithmetic: 0.98 us -> none  [the longest x1 0.67 us: on_device(): jnp.sum(jnp.where(both & (earlier == n), order + 1, 0))]
  transfers between devices with their start and end apart: 5 -> 5, of which waited for: 2 -> 2; matrix products, arithmetic and copies ran while one was open for 4% -> 0% of each run, Pallas kernels for 14% -> 13%
where the time goes in v2:
time: 87.7 us; the launch traced here: 87.3 us
  waiting for transfers between devices  43.2 us (49%)
  starting transfers between devices  22.8 us (26%)
  Pallas kernels  18.4 us (21%)
  between operations  1.62 us (2%)
    all_to_all x1, waiting for transfers between devices, finish(): got = lax.all_to_all(send, 'dp', split_axis=0, concat_axis=0, tiled=True)  40 us
    all_to_all x1, starting transfers between devices, finish(): got = lax.all_to_all(send, 'dp', split_axis=0, concat_axis=0, tiled=True)  9.73 us
    ppermute x3, starting transfers between devices, shifted(): return lax.ppermute(message, 'dp', pairs)  9.11 us
    pallas_call x1, Pallas kernels, on_device(): pl.pallas_call(added_kernel, in_specs=[HBM] * 7, out_specs=[HBM] * 8 + [p...  4.72 us
    pallas_call x1, Pallas kernels, finish(): pl.pallas_call(gate_kernel, in_specs=[HBM] * 6 + [ANY], out_specs=[HBM] *...  4.66 us
    all_to_all x1, starting transfers between devices, finish(): lax.all_to_all(squares, 'tensor', split_axis=0, concat_axis=0, axis_index...  3.99 us
    pallas_call x1, Pallas kernels, finish(): pl.pallas_call(within_kernel, in_specs=[HBM] * 7, out_specs=[VMEM] * 3, o...  3.9 us
    all_to_all x1, waiting for transfers between devices, finish(): lax.all_to_all(squares, 'tensor', split_axis=0, concat_axis=0, axis_index...  3.24 us
  transfers between devices with their start and end apart: 5, of which 2 were waited for; matrix products, arithmetic and copies ran while one was open for 0% of the time, Pallas kernels for 13%

profile of v2, /device:TPU:32, one launch (start us, length us, event | category | flops | bytes accessed | tf_op | source)
XLA Modules:
  0.0 87.3 jit_solution(616254111226537424)
XLA Ops:
  0.6 0.0 copy-start.10
  0.6 0.0 copy-start.12
  0.7 0.0 copy-start.2
  0.7 0.0 copy-start.1
  0.7 0.0 copy-start.13
  0.7 0.0 copy-start
  0.7 0.0 copy-start.11
  0.7 4.7 %added.1 = (bf16[16,272,256]{2,1,0:T(8,128)(2,1)}, bf16[272,256]{1,0:T(8,128)(2,1)}, bf16[272,256]{1,0:T(8,128)(2,1)}, bf16[272,256]{1,0:T(8,128)(2,1)}, bf16[27...) custom-call(s32[128]{0:T(128)} %dest_hbm.1, ...), custom_call_target="tpu_custom_call" | custom-call | tf_op jit(solution)/shard_map/added/pallas_call | solution.py:521
  6.1 0.0 copy-done.10
  6.1 0.0 copy-done.12
  6.1 0.0 copy-done.2
  6.1 0.0 copy-done.1
  6.1 0.0 copy-done.13
  6.1 0.0 copy-done
  6.1 0.0 copy-done.11
  6.1 80.9 %conditional.6 = (bf16[8,128,256]{2,1,0:T(8,128)(2,1)}, bf16[8,4,64,256]{3,2,1,0:T(8,128)(2,1)}) conditional(s32[]{:T(128)} %bitcast.13, (f32[4]{0:T(128)S(1)}, f32[4]{0:T(128)S(1)}, bf16[8,128,256]{2,1,0:T(8,128)(2,1)}, bf16[8,128,1024]{2,1,0:T(8,128)(2,1)}, bf16[8,128,1024]{2,1,0:T(8,128)(2,1)S(1)}, ...), branch_computations={%region_0.0_spmd, %region_1.8_spmd, %region_8.14_spmd, %region_14.... | conditional | flops 4 | bytes 10813910 | solution.py:546
  6.2 9.7 %all-to-all-start = ((bf16[16,272,256]{2,1,0:T(8,128)(2,1)}), bf16[16,272,256]{2,1,0:T(8,128)(2,1)}, u32[]{:S(2)}, u32[]{:S(2)}) async-start(bf16[16,272,256]{2,1,0:T(8,128)(2,1)} %get-tuple-element.338), calls=%async_computation | async-start | bytes 4456448 | tf_op jit(solution)/shard_map/cond/branch_0_fun/all_to_all | solution.py:400
  15.9 2.1 %collective-permute-start = (bf16[272,256]{1,0:T(8,128)(2,1)}, bf16[272,256]{1,0:T(8,128)(2,1)}, u32[]{:S(2)}, u32[]{:S(2)}) collective-permute-start(bf16[272,256]{1,0:T(8,128)(2,1)} %get-tuple-element.342), channel_id=1, source_target_pairs={{0,256},{32,288},{64,320},{96,352},{128,384},{160,416},{192,448},{... | collective-permute-start | bytes 417800 | tf_op jit(solution)/shard_map/cond/branch_0_fun/ppermute | solution.py:377
  18.0 1.9 %collective-permute-start.1 = (bf16[272,256]{1,0:T(8,128)(2,1)}, bf16[272,256]{1,0:T(8,128)(2,1)}, u32[]{:S(2)}, u32[]{:S(2)}) collective-permute-start(bf16[272,256]{1,0:T(8,128)(2,1)} %get-tuple-element.343), channel_id=1, source_target_pairs={{0,32},{32,0},{64,96},{96,64},{128,160},{160,128},{192,224},{224,1... | collective-permute-start | bytes 417800 | tf_op jit(solution)/shard_map/cond/branch_0_fun/ppermute | solution.py:377
  20.0 5.1 %collective-permute-start.2 = (bf16[272,256]{1,0:T(8,128)(2,1)}, bf16[272,256]{1,0:T(8,128)(2,1)}, u32[]{:S(2)}, u32[]{:S(2)}) collective-permute-start(bf16[272,256]{1,0:T(8,128)(2,1)} %get-tuple-element.344), channel_id=1, source_target_pairs={{0,480},{32,64},{64,32},{96,128},{128,96},{160,192},{192,160},{224... | collective-permute-start | bytes 417800 | tf_op jit(solution)/shard_map/cond/branch_0_fun/ppermute | solution.py:377
  25.0 3.9 %within.7 = (f32[8,128,256]{2,1,0:T(8,128)}, f32[128,32]{1,0:T(8,128)}, f32[8,128,256]{2,1,0:T(8,128)}) custom-call(f32[4]{0:T(128)S(1)} %get-tuple-element.328.a_hbm, f32[4]{0:T(128)S(1)} %get-tuple-element.329.d_hbm, bf16[8,128,256]{2,1,0:T(8,128)(2,1)} %get-tuple-element.330.x_hbm, bf16[8,128,1024]{2,1,0:T(8,128)(2,1)} %get-tuple-element.331.b_hbm, ...), custom_call_target="tpu_custom_call" | custom-call | tf_op jit(solution)/shard_map/cond/branch_0_fun/within/pallas_call | solution.py:402
  28.9 40.0 %all-to-all-done.got = bf16[16,272,256]{2,1,0:T(8,128)(2,1)} async-done(((bf16[16,272,256]{2,1,0:T(8,128)(2,1)}), bf16[16,272,256]{2,1,0:T(8,128)(2,1)}, u32[]{:S(2)}, u32[]{:S(2)}) %all-to-all-start) | async-done | bytes 2228256 | tf_op jit(solution)/shard_map/cond/branch_0_fun/all_to_all | solution.py:400
  68.9 4.7 %gate.7 = (f32[8,128,256]{2,1,0:T(8,128)}, f32[8,8,128]{2,1,0:T(8,128)}) custom-call(s32[128]{0:T(128)S(1)} %get-tuple-element.326.dest_hbm, bf16[8,128,1024]{2,1,0:T(8,128)(2,1)S(1)} %get-tuple-element.327.c_hbm, f32[8,128,256]{2,1,0:T(8,128)} %get-tuple-element.334.silu_hbm, f32[8,128,256]{2,1,0:T(8,128)} %get-tuple-element.335.within_hbm, ...), custom_call_target="tpu_custom_call" | custom-call | tf_op jit(solution)/shard_map/cond/branch_0_fun/gate/pallas_call | solution.py:439
  73.6 4.0 %all-to-all-start.1 = ((f32[8,8,128]{2,1,0:T(8,128)}), f32[8,8,128]{2,1,0:T(8,128)S(1)}, u32[]{:S(2)}, u32[]{:S(2)}) async-start(f32[8,8,128]{2,1,0:T(8,128)} %get-tuple-element.340), calls=%async_computation.1 | async-start | bytes 65536 | tf_op jit(solution)/shard_map/cond/branch_0_fun/all_to_all | solution.py:466
  77.6 0.0 collective-permute-done.rest_0_
  77.6 0.0 collective-permute-done.1.rest_1_
  77.6 0.0 collective-permute-done.2.rest_2_
  77.6 3.0 %new_states.7 = bf16[8,256,256]{2,1,0:T(8,128)(2,1)} custom-call(s32[128]{0:T(128)S(1)} %get-tuple-element.326.dest_hbm, bf16[8,256,256]{2,1,0:T(8,128)(2,1)S(1)} %get-tuple-element.337.states_hbm, bf16[16,272,256]{2,1,0:T(8,128)(2,1)} %all-to-all-done.got, bf16[272,256]{1,0:T(8,128)(2,1)} %collective-permute-done.rest_0_, ...), custom_call_target="tpu_custom_call" | custom-call | tf_op jit(solution)/shard_map/cond/branch_0_fun/new_states/pallas_call | solution.py:470
  80.6 3.2 %all-to-all-done.1.squares_hbm = f32[8,8,128]{2,1,0:T(8,128)S(1)} async-done(((f32[8,8,128]{2,1,0:T(8,128)}), f32[8,8,128]{2,1,0:T(8,128)S(1)}, u32[]{:S(2)}, u32[]{:S(2)}) %all-to-all-start.1) | async-done | bytes 32800 | tf_op jit(solution)/shard_map/cond/branch_0_fun/all_to_all | solution.py:466
  83.8 0.0 copy-start.9
  83.8 0.6 copy-done.9
  84.4 2.1 %norm.7 = bf16[8,128,256]{2,1,0:T(8,128)(2,1)} custom-call(f32[8,128,256]{2,1,0:T(8,128)} %get-tuple-element.339.gated_hbm, f32[8,8,128]{2,1,0:T(8,128)} %copy-done.9, f32[1,256]{1,0:T(1,128)S(1)} %get-tuple-element.341.gain_hbm), custom_call_target="tpu_custom_call" | custom-call | tf_op jit(solution)/shard_map/cond/branch_0_fun/norm/pallas_call | solution.py:489
Async XLA Ops:
  0.6 5.4 %copy-start.10 = (s32[128]{0:T(128)S(1)}, s32[128]{0:T(128)}, u32[]{:S(2)}) copy-start(s32[128]{0:T(128)} %dest_hbm.1) | copy-start | bytes 1540
  0.6 5.4 %copy-start.12 = (f32[4]{0:T(128)S(1)}, f32[4]{0:T(128)}, u32[]{:S(2)}) copy-start(f32[4]{0:T(128)} %a_hbm.1) | copy-start | bytes 52
  0.7 5.4 %copy-start.2 = (f32[8,4,128]{2,1,0:T(4,128)S(1)}, f32[8,4,128]{2,1,0:T(4,128)}, u32[]{:S(2)}) copy-start(f32[8,4,128]{2,1,0:T(4,128)} %dt_hbm.1) | copy-start | bytes 49156
  0.7 5.4 %copy-start.1 = (bf16[8,4,64,256]{3,2,1,0:T(8,128)(2,1)S(1)}, bf16[8,4,64,256]{3,2,1,0:T(8,128)(2,1)}, u32[]{:S(2)}) copy-start(bf16[8,4,64,256]{3,2,1,0:T(8,128)(2,1)} %param.46) | copy-start | bytes 3145732
  0.7 5.4 %copy-start.13 = (f32[4]{0:T(128)S(1)}, f32[4]{0:T(128)}, u32[]{:S(2)}) copy-start(f32[4]{0:T(128)} %param.44) | copy-start | bytes 52
  0.7 5.4 %copy-start = (bf16[8,128,1024]{2,1,0:T(8,128)(2,1)S(1)}, bf16[8,128,1024]{2,1,0:T(8,128)(2,1)}, u32[]{:S(2)}) copy-start(bf16[8,128,1024]{2,1,0:T(8,128)(2,1)} %param.41) | copy-start | bytes 6291460
  0.7 5.4 %copy-start.11 = (f32[256]{0:T(256)S(1)}, f32[256]{0:T(256)}, u32[]{:S(2)}) copy-start(f32[256]{0:T(256)} %param.45) | copy-start | bytes 3076
  6.2 62.7 %all-to-all-start = ((bf16[16,272,256]{2,1,0:T(8,128)(2,1)}), bf16[16,272,256]{2,1,0:T(8,128)(2,1)}, u32[]{:S(2)}, u32[]{:S(2)}) async-start(bf16[16,272,256]{2,1,0:T(8,128)(2,1)} %get-tuple-element.338), calls=%async_computation | async-start | bytes 4456448 | tf_op jit(solution)/shard_map/cond/branch_0_fun/all_to_all | solution.py:400
  15.9 61.7 %collective-permute-start = (bf16[272,256]{1,0:T(8,128)(2,1)}, bf16[272,256]{1,0:T(8,128)(2,1)}, u32[]{:S(2)}, u32[]{:S(2)}) collective-permute-start(bf16[272,256]{1,0:T(8,128)(2,1)} %get-tuple-element.342), channel_id=1, source_target_pairs={{0,256},{32,288},{64,320},{96,352},{128,384},{160,416},{192,448},{... | collective-permute-start | bytes 417800 | tf_op jit(solution)/shard_map/cond/branch_0_fun/ppermute | solution.py:377
  18.0 59.5 %collective-permute-start.1 = (bf16[272,256]{1,0:T(8,128)(2,1)}, bf16[272,256]{1,0:T(8,128)(2,1)}, u32[]{:S(2)}, u32[]{:S(2)}) collective-permute-start(bf16[272,256]{1,0:T(8,128)(2,1)} %get-tuple-element.343), channel_id=1, source_target_pairs={{0,32},{32,0},{64,96},{96,64},{128,160},{160,128},{192,224},{224,1... | collective-permute-start | bytes 417800 | tf_op jit(solution)/shard_map/cond/branch_0_fun/ppermute | solution.py:377
  20.0 57.6 %collective-permute-start.2 = (bf16[272,256]{1,0:T(8,128)(2,1)}, bf16[272,256]{1,0:T(8,128)(2,1)}, u32[]{:S(2)}, u32[]{:S(2)}) collective-permute-start(bf16[272,256]{1,0:T(8,128)(2,1)} %get-tuple-element.344), channel_id=1, source_target_pairs={{0,480},{32,64},{64,32},{96,128},{128,96},{160,192},{192,160},{224... | collective-permute-start | bytes 417800 | tf_op jit(solution)/shard_map/cond/branch_0_fun/ppermute | solution.py:377
  73.6 10.2 %all-to-all-start.1 = ((f32[8,8,128]{2,1,0:T(8,128)}), f32[8,8,128]{2,1,0:T(8,128)S(1)}, u32[]{:S(2)}, u32[]{:S(2)}) async-start(f32[8,8,128]{2,1,0:T(8,128)} %get-tuple-element.340), calls=%async_computation.1 | async-start | bytes 65536 | tf_op jit(solution)/shard_map/cond/branch_0_fun/all_to_all | solution.py:466
  83.8 0.6 copy-start.9
